TPU v7x, 32 devices: a whole 2x2x4 slice. The times are simulated.
32 devices in a mesh: section: 4 (over z), ctx: 8 (over y, x, core).
Axes of the slice: x: 2, y: 2, z: 4, core: 2. Of those that a mesh axis runs over, the one named last changes fastest.
Arguments:
- queries: bfloat16 [8, 1280, 3072], P('section', 'ctx'), may hold values from -28 to 28, as said below
- cotangent: bfloat16 [8, 1280, 3072], P('section', 'ctx'), may hold values from -6 to 6
- ret_query: bfloat16 [1280, 3072], P('ctx', 'section'), may hold values from -6 to 6
- ret_key: bfloat16 [1280, 3072], P('ctx', 'section'), may hold values from -6 to 6
- ret_value: bfloat16 [1280, 3072], P('ctx', 'section'), may hold values from -6 to 6
- gate_log: float32 [1280, 24], P('ctx', 'section'), may hold values from -1.5 to 0, as said below
- kv_weight: bfloat16 [3072, 2048], P('section'), may hold values from -0.109375 to 0.109375
Outputs:
- attention: bfloat16 [8, 1280, 3072], P('section', 'ctx')
- query_grad: bfloat16 [8, 1280, 3072], P('section', 'ctx')
- retention_grad: bfloat16 [1280, 3072], P('ctx', 'section')
Inputs may be any that keep to these rules, and one draw needn't show every extreme that they name: The attention queries are mostly of order one; a few rows may be scaled by up to 16. `gate_log`: every gate is below one.
All inputs are finite; a program needn't handle non-finite values.
Results may differ from a plain program's by a relative error of at most 0.034.
Values may be sent and summed in bfloat16 or wider, within the bound.
A program may use at most 640 MiB of HBM per device.

v0:
```python
import math

import jax
import jax.numpy as jnp
from jax import lax
from jax.sharding import PartitionSpec as P

DH = 128


epsilon = 1e-06
highest = lax.Precision.HIGHEST


def entering(value, axis, join, neutral):
    count, mine = (lax.axis_size(axis), lax.axis_index(axis))
    pieces = jax.tree.map(lambda part: lax.all_gather(part, axis), value)
    running = jax.tree.map(
        lambda part, zero: jnp.full_like(part, 0) + jnp.asarray(zero, part.dtype), value, neutral
    )

    def lap(position, running):
        longer = join(running, jax.tree.map(lambda part: part[position], pieces))
        return jax.tree.map(lambda new, old: jnp.where(position < mine, new, old), longer, running)

    return lax.fori_loop(0, count - 1, lap, running)


def combine_state(earlier, later):
    return (earlier[0] * later[0], later[0][:, None, None] * earlier[1] + later[1])


def kept_memory_lines(ret_query, ret_key, ret_value, gate_log):
    row_count, heads_here = gate_log.shape
    head_width = ret_query.shape[1] // heads_here
    query_part = ret_query.astype(jnp.float32).reshape(row_count, heads_here, head_width)
    key_part = ret_key.astype(jnp.float32).reshape(row_count, heads_here, head_width)
    value_part = ret_value.astype(jnp.float32).reshape(row_count, heads_here, head_width)
    cumulative = jnp.cumsum(gate_log, axis=0)
    places = jnp.arange(row_count, dtype=jnp.int32)
    causal = places[:, None] >= places[None, :]
    spread = cumulative.T[:, :, None] - cumulative.T[:, None, :]
    weights = jnp.exp(jnp.where(causal[None], spread, -jnp.inf))
    scores = jnp.einsum("thd,uhd->htu", query_part, key_part, precision=highest)
    inside = jnp.einsum("htu,uhd->thd", weights * scores, value_part, precision=highest)
    tail_decay = jnp.exp(cumulative[-1][None, :] - cumulative)
    local_state = jnp.einsum("uh,uhd,uhe->hde", tail_decay, key_part, value_part, precision=highest)
    decay_total = jnp.exp(cumulative[-1])
    identity = (jnp.ones_like(decay_total), jnp.zeros_like(local_state))
    scanned = entering((decay_total, local_state), "ctx", combine_state, identity)
    state_before = scanned[1]
    carried = jnp.einsum("thd,hde->the", query_part, state_before, precision=highest)
    raw_output = inside + jnp.exp(cumulative)[:, :, None] * carried
    normed = raw_output * lax.rsqrt(
        jnp.mean(raw_output * raw_output, axis=-1, keepdims=True) + epsilon
    )
    return normed.astype(jnp.bfloat16).reshape(row_count, heads_here * head_width)


def cross_attention(query_rows, grad_rows, positions, full_cache):
    row_count, model_width = query_rows.shape
    kv_width = full_cache.shape[1] // 2
    head_width = DH
    kv_heads = kv_width // head_width
    group_size = model_width // kv_width
    total_rows = full_cache.shape[0]
    block_rows = math.gcd(512, total_rows)
    score_scale = 1.0 / math.sqrt(head_width)
    query_heads = query_rows.reshape(row_count, kv_heads, group_size, head_width)
    grad_heads = grad_rows.reshape(row_count, kv_heads, group_size, head_width)
    block_count = jnp.max(positions) // block_rows + 1

    def block_scores(block_index):
        first_row = block_index * block_rows
        cache_piece = lax.dynamic_slice_in_dim(full_cache, first_row, block_rows, 0)
        key_block = cache_piece[:, :kv_width].reshape(block_rows, kv_heads, head_width)
        value_block = cache_piece[:, kv_width:].reshape(block_rows, kv_heads, head_width)
        scores = (
            jnp.einsum("rkgd,ukd->kgru", query_heads, key_block, preferred_element_type=jnp.float32)
            * score_scale
        )
        visible = (
            positions[:, None] >= (first_row + jnp.arange(block_rows, dtype=jnp.int32))[None, :]
        )
        return (jnp.where(visible, scores, -jnp.inf), key_block, value_block)

    def stat_step(block_index, carried):
        row_top, row_total = carried
        scores = block_scores(block_index)[0]
        new_top = jnp.maximum(row_top, jnp.max(scores, axis=-1))
        row_total = row_total * jnp.exp(row_top - new_top) + jnp.sum(
            jnp.exp(scores - new_top[..., None]), axis=-1
        )
        return (new_top, row_total)

    start_top = jnp.full((kv_heads, group_size, row_count), -jnp.inf, jnp.float32)
    row_top, row_total = lax.fori_loop(
        0, block_count, stat_step, (start_top, jnp.zeros_like(start_top))
    )

    def soft_of(scores):
        return jnp.exp(scores - row_top[..., None]) / row_total[..., None]

    def forward_step(block_index, accumulated):
        scores, _, value_block = block_scores(block_index)
        probs_low = soft_of(scores).astype(jnp.bfloat16)
        return accumulated + jnp.einsum(
            "kgru,ukd->rkgd", probs_low, value_block, preferred_element_type=jnp.float32
        )

    start_out = jnp.zeros((row_count, kv_heads, group_size, head_width), jnp.float32)
    mixed_output = lax.fori_loop(0, block_count, forward_step, start_out).astype(jnp.bfloat16)
    row_delta = jnp.einsum(
        "rkgd,rkgd->kgr", grad_heads, mixed_output, preferred_element_type=jnp.float32
    )

    def backward_step(block_index, carried):
        query_grad, cache_term = carried
        scores, key_block, value_block = block_scores(block_index)
        soft_probs = soft_of(scores)
        probs_low = soft_probs.astype(jnp.bfloat16)
        prob_grad = jnp.einsum(
            "rkgd,ukd->kgru", grad_heads, value_block, preferred_element_type=jnp.float32
        )
        score_grad = (soft_probs * (prob_grad - row_delta[..., None]) * score_scale).astype(
            jnp.bfloat16
        )
        query_grad = query_grad + jnp.einsum(
            "kgru,ukd->rkgd", score_grad, key_block, preferred_element_type=jnp.float32
        )
        key_grad = jnp.einsum(
            "kgru,rkgd->ukd", score_grad, query_heads, preferred_element_type=jnp.float32
        )
        value_grad = jnp.einsum(
            "kgru,rkgd->ukd", probs_low, grad_heads, preferred_element_type=jnp.float32
        )
        rows_term = jnp.concatenate(
            [key_grad.reshape(block_rows, kv_width), value_grad.reshape(block_rows, kv_width)],
            axis=1,
        )
        first_row = block_index * block_rows
        before = lax.dynamic_slice_in_dim(cache_term, first_row, block_rows, 0)
        cache_term = lax.dynamic_update_slice_in_dim(cache_term, before + rows_term, first_row, 0)
        return (query_grad, cache_term)

    start_term = jnp.zeros((total_rows, 2 * kv_width), jnp.float32)
    query_grad, cache_term = lax.fori_loop(0, block_count, backward_step, (start_out, start_term))
    return (
        mixed_output.reshape(row_count, model_width),
        query_grad.astype(jnp.bfloat16).reshape(row_count, model_width),
        cache_term,
    )


def body(queries, cotangent, ret_query, ret_key, ret_value, gate_log, kv_weight):
    ret_out = kept_memory_lines(ret_query, ret_key, ret_value, gate_log)
    partial_rows = jnp.dot(ret_out, kv_weight, preferred_element_type=jnp.float32)
    cache = lax.psum(partial_rows, "section").astype(jnp.bfloat16)
    full_cache = lax.all_gather(cache, "ctx", axis=0, tiled=True)
    layer_count, own_count, model_width = queries.shape
    ctx_place = lax.axis_index("ctx")
    local_rows = jnp.arange(own_count, dtype=jnp.int32)
    total_rows = full_cache.shape[0]
    term_width = full_cache.shape[1]
    cache_total = jnp.zeros((total_rows, term_width), jnp.float32)
    attended_list = []
    grad_list = []
    positions = ctx_place * own_count + local_rows
    for layer in range(layer_count):
        mixed_output, query_grad, cache_term = cross_attention(
            queries[layer], cotangent[layer], positions, full_cache
        )
        cache_total = cache_total + cache_term
        attended_list.append(mixed_output)
        grad_list.append(query_grad)
    attended_all = jnp.stack(attended_list, axis=0)
    grad_rows_all = jnp.stack(grad_list, axis=0)
    own_part = lax.psum_scatter(cache_total, "ctx", scatter_dimension=0, tiled=True)
    summed_grad = lax.psum(own_part, "section")
    cache_grad = summed_grad.astype(jnp.bfloat16)
    retention_grad = jnp.einsum(
        "rw,cw->rc", cache_grad, kv_weight, preferred_element_type=jnp.float32
    ).astype(jnp.bfloat16)
    return (attended_all, grad_rows_all, retention_grad)


def solution(mesh):
    return jax.shard_map(
        body,
        mesh=mesh,
        in_specs=(
            P("section", "ctx", None),
            P("section", "ctx", None),
            P("ctx", "section"),
            P("ctx", "section"),
            P("ctx", "section"),
            P("ctx", "section"),
            P("section", None),
        ),
        out_specs=(P("section", "ctx", None), P("section", "ctx", None), P("ctx", "section")),
        check_vma=False,
    )
```

profile of v0, /device:TPU:0, one launch (start us, length us, event | category | flops | bytes accessed | tf_op | source)
XLA Modules:
  0.0 642.8 jit_solution(4108917119197346876)
XLA Ops:
  15.9 10.3 %all-gather.1 = f32[8,1,6]{2,1,0:T(1,128)S(1)} all-gather(f32[1,1,6]{2,1,0:T(1,128)} %bitcast.401), channel_id=1, replica_groups=mesh['section'=4,'ctx'=8] {'ctx'}, dimensions={0}, use_global_device_ids=true | all-gather | bytes 216 | tf_op jit(solution)/shard_map/all_gather | solution.py:17
  28.6 22.4 %all-gather.7.cloned.1.call-done = f32[48,128,128]{2,1,0:T(8,128)} async-done(((f32[6,128,128]{2,1,0:T(8,128)}), f32[48,128,128]{2,1,0:T(8,128)}) %all-gather.7.cloned.1.call-update) | async-done | bytes 3145744 | tf_op jit(solution)/shard_map/all_gather | solution.py:17
  51.0 8.1 %while.94 = (s32[]{:T(128)}, f32[6,128,128]{2,1,0:T(8,128)S(1)}, s32[]{:T(128)}, f32[8,6]{1,0:T(8,128)S(1)}, f32[8,6,128,128]{3,2,1,0:T(8,128)}, /*index=5*/s32[]{:T(128)}, s32[]{:T(128)}) while((s32[]{:T(128)}, f32[6,128,128]{2,1,0:T(8,128)S(1)}, s32[]{:T(128)}, f32[8,6]{1,0:T(8,128)S(1)}, f32[8,6,128,128]{3,2,1,0:T(8,128)}, ...), condition=%wide.region_4.5_spmd.clone, body=%wide.region_3.4_spmd.clone.sunk | while | flops 393220 | bytes 1179833 | solution.py:26
  64.2 53.5 %all-reduce.3 = bf16[160,2048]{1,0:T(8,128)(2,1)} all-reduce(f32[160,2048]{1,0:T(8,128)} %fusion.51), channel_id=1, replica_groups=mesh['section'=4,'ctx'=8] {'section'}, use_global_device_ids=true, to_apply=%region_6.7 | all-reduce | flops 327680 | bytes 1966080 | tf_op jit(solution)/shard_map/psum | solution.py:158
  139.0 4.0 reshape_squeeze.14
  152.5 4.1 all-gather.5.cloned.1.call-done
  156.6 7.9 %copy.212 = bf16[1280,2048]{0,1:T(8,128)(2,1)} copy(bf16[1280,2048]{1,0:T(8,128)(2,1)} %all-gather.5.cloned.1.call-done) | data formatting | bytes 10485760
  164.6 5.6 while.88
  171.7 6.9 %while.89 = (s32[]{:T(128)}, f32[160,8,3,128]{3,0,2,1:T(8,128)}, s32[]{:T(128)}, bf16[1280,2048]{0,1:T(8,128)(2,1)}, bf16[160,8,3,128]{3,0,2,1:T(8,128)(2,1)}, /...) while((s32[]{:T(128)}, f32[160,8,3,128]{3,0,2,1:T(8,128)}, ...), condition=%wide.region_12.13_spmd.clone, body=%wide.region_11.12_spmd.clone.sunk | while | flops 508764576 | bytes 8177095 | solution.py:112
  174.0 4.5 bitcast_add_fusion.9
  182.0 5.4 while.90
  189.0 7.0 %while.91 = (s32[]{:T(128)}, f32[160,8,3,128]{3,0,2,1:T(8,128)}, s32[]{:T(128)}, bf16[1280,2048]{0,1:T(8,128)(2,1)}, bf16[160,8,3,128]{3,0,2,1:T(8,128)(2,1)}, /...) while((s32[]{:T(128)}, f32[160,8,3,128]{3,0,2,1:T(8,128)}, ...), condition=%wide.region_18.19_spmd.clone, body=%wide.region_17.18_spmd.clone.sunk | while | flops 508764576 | bytes 8177095 | solution.py:112
  191.3 4.5 bitcast_add_fusion.10
  203.7 4.6 multiply_reduce_fusion
  211.2 4.7 broadcast.119.clone
  215.8 12.6 %while.93 = (s32[]{:T(128)}, f32[160,8,3,128]{3,0,2,1:T(8,128)}, f32[1280,2048]{0,1:T(8,128)}, s32[]{:T(128)}, bf16[1280,2048]{0,1:T(8,128)(2,1)}, /*index=5*/bf...) while((s32[]{:T(128)}, f32[160,8,3,128]{3,0,2,1:T(8,128)}, ...), condition=%wide.region_22.23_spmd.clone, body=%wide.region_21.22_spmd.clone.sunk | while | flops 1268720000 | bytes 61342288 | solution.py:147
  224.4 4.0 fusion.198
  230.0 4.5 broadcast.119.clone.1
  234.5 12.8 %while.92 = (s32[]{:T(128)}, f32[160,8,3,128]{3,0,2,1:T(8,128)}, f32[1280,2048]{0,1:T(8,128)}, s32[]{:T(128)}, bf16[1280,2048]{0,1:T(8,128)(2,1)}, /*index=5*/bf...) while((s32[]{:T(128)}, f32[160,8,3,128]{3,0,2,1:T(8,128)}, ...), condition=%wide.region_20.21_spmd.clone, body=%wide.region_19.20_spmd.clone.sunk | while | flops 1268720000 | bytes 61342288 | solution.py:147
  247.3 12.2 %add.195 = f32[1280,2048]{0,1:T(8,128)} add(f32[1280,2048]{0,1:T(8,128)} %get-tuple-element.388, f32[1280,2048]{0,1:T(8,128)} %get-tuple-element.389) | non-fusion elementwise | flops 2621440 | bytes 31457280 | tf_op jit(solution)/shard_map/add | solution.py:173
  259.6 11.4 %copy.282 = f32[1280,2048]{1,0:T(8,128)} copy(f32[1280,2048]{0,1:T(8,128)} %add.195) | data formatting | bytes 20971520
  298.4 4.4 pad_maximum_fusion
  302.8 249.0 %reduce-scatter.4.cloned.1.call-done = f32[160,2048]{1,0:T(8,128)} async-done(((f32[1280,2048]{1,0:T(8,128)}), f32[160,2048]{1,0:T(8,128)}) %reduce-scatter.4.cloned.1.call-update) | async-done | bytes 1310736
  554.6 78.1 %all-reduce.4 = bf16[160,2048]{0,1:T(8,128)(2,1)} all-reduce(f32[160,2048]{0,1:T(8,128)} %copy.283), channel_id=1, replica_groups=mesh['section'=4,'ctx'=8] {'section'}, use_global_device_ids=true, to_apply=%region_24.25 | all-reduce | flops 327680 | bytes 1966080 | tf_op jit(solution)/shard_map/psum | solution.py:179
  (149 shorter events, 140.5 us)
Async XLA Ops:
  7.2 55.2 %copy-start = (bf16[768,2048]{1,0:T(8,128)(2,1)S(1)}, bf16[768,2048]{1,0:T(8,128)(2,1)}, u32[]{:S(2)}) copy-start(bf16[768,2048]{1,0:T(8,128)(2,1)} %param.27) | copy-start | bytes 9437188
  7.2 43.8 %all-gather.7.cloned.1.call-start = ((), (), s32[]{:S(2)}) async-start(), calls=%async_computation.2 | async-start | bytes 3538944 | tf_op jit(solution)/shard_map/all_gather | solution.py:17
  15.8 140.8 %all-gather.5.cloned.1.call-start = ((), (), s32[]{:S(2)}) async-start(), calls=%async_computation.1 | async-start | bytes 5898240 | tf_op jit(solution)/shard_map/all_gather | solution.py:159
  28.6 30.4 %copy-start.12 = (f32[160,6]{0,1:T(8,128)S(1)}, f32[160,6]{0,1:T(8,128)}, u32[]{:S(2)}) copy-start(f32[160,6]{0,1:T(8,128)} %get-tuple-element.949) | copy-start | bytes 11524
  117.8 434.0 %reduce-scatter.4.cloned.1.call-start = ((), (), s32[]{:S(2)}) async-start(), calls=%async_computation.3 | async-start | bytes 11796480
  134.8 2.9 copy-start.11
  196.0 3.7 copy-start.9
  196.0 3.7 copy-start.10
  217.2 3.3 copy-start.2
  221.1 1.2 copy-start.4
  222.0 1.6 copy-start.7
  224.4 4.0 copy-start.8
  236.1 3.3 copy-start.1
  240.0 1.2 copy-start.3
  240.9 1.6 copy-start.5
  243.3 4.0 copy-start.6
Sparse Core Ops, SparseCore 0:
  15.9 34.9 all-gather.6
  117.9 38.6 all-gather.4
  271.1 280.6 reduce-scatter.3
where the time goes:
time: 655 us; the launch traced here: 643 us
  waiting for transfers between devices  276 us (42%)
  blocking collectives  142 us (22%)
  local copies, waits for them, and re-layouts  110 us (17%)
  other arithmetic  57.6 us (9%)
  matrix products  39.1 us (6%)
  between operations  17 us (3%)
    unnamed x4, waiting for transfers between devices  249 us
    psum x1, blocking collectives, body(): summed_grad = lax.psum(own_part, 'section')  78.1 us
    psum x1, blocking collectives, body(): cache = lax.psum(partial_rows, 'section').astype(jnp.bfloat16)  53.5 us
    unnamed x18, local copies, waits for them, and re-layouts  33.3 us
    all_gather x1, waiting for transfers between devices, entering(): pieces = jax.tree.map(lambda part: lax.all_gather(part, axis), value)  22.4 us
    another operation x12, local copies, waits for them, and re-layouts  15.3 us
    unnamed x6, other arithmetic  14.4 us
  transfers between devices with their start and end apart: 3, of which 3 were waited for; matrix products, arithmetic and copies ran while one was open for 10% of the time, Pallas kernels for 0%

commit v1 on v0

v1 whole, which is shorter than its diff:
```python
import math

import jax
import jax.numpy as jnp
from jax import lax
from jax.experimental import pallas as pl
from jax.experimental.pallas import tpu as pltpu
from jax.sharding import PartitionSpec as P

DH = 128


epsilon = 1e-06
highest = lax.Precision.HIGHEST


def entering(value, axis, join, neutral):
    count, mine = (lax.axis_size(axis), lax.axis_index(axis))
    pieces = jax.tree.map(lambda part: lax.all_gather(part, axis), value)
    running = jax.tree.map(
        lambda part, zero: jnp.full_like(part, 0) + jnp.asarray(zero, part.dtype), value, neutral
    )

    def lap(position, running):
        longer = join(running, jax.tree.map(lambda part: part[position], pieces))
        return jax.tree.map(lambda new, old: jnp.where(position < mine, new, old), longer, running)

    return lax.fori_loop(0, count - 1, lap, running)


def combine_state(earlier, later):
    return (earlier[0] * later[0], later[0][:, None, None] * earlier[1] + later[1])


def kept_memory_lines(ret_query, ret_key, ret_value, gate_log):
    row_count, heads_here = gate_log.shape
    head_width = ret_query.shape[1] // heads_here
    query_part = ret_query.astype(jnp.float32).reshape(row_count, heads_here, head_width)
    key_part = ret_key.astype(jnp.float32).reshape(row_count, heads_here, head_width)
    value_part = ret_value.astype(jnp.float32).reshape(row_count, heads_here, head_width)
    cumulative = jnp.cumsum(gate_log, axis=0)
    places = jnp.arange(row_count, dtype=jnp.int32)
    causal = places[:, None] >= places[None, :]
    spread = cumulative.T[:, :, None] - cumulative.T[:, None, :]
    weights = jnp.exp(jnp.where(causal[None], spread, -jnp.inf))
    scores = jnp.einsum("thd,uhd->htu", query_part, key_part, precision=highest)
    inside = jnp.einsum("htu,uhd->thd", weights * scores, value_part, precision=highest)
    tail_decay = jnp.exp(cumulative[-1][None, :] - cumulative)
    local_state = jnp.einsum("uh,uhd,uhe->hde", tail_decay, key_part, value_part, precision=highest)
    decay_total = jnp.exp(cumulative[-1])
    identity = (jnp.ones_like(decay_total), jnp.zeros_like(local_state))
    scanned = entering((decay_total, local_state), "ctx", combine_state, identity)
    state_before = scanned[1]
    carried = jnp.einsum("thd,hde->the", query_part, state_before, precision=highest)
    raw_output = inside + jnp.exp(cumulative)[:, :, None] * carried
    normed = raw_output * lax.rsqrt(
        jnp.mean(raw_output * raw_output, axis=-1, keepdims=True) + epsilon
    )
    return normed.astype(jnp.bfloat16).reshape(row_count, heads_here * head_width)


def attention_kernel(ctx_ref, q_ref, g_ref, k_ref, v_ref, att_ref, qg_ref, kg_ref, vg_ref):
    layer_count, row_count, width = q_ref.shape
    group = width // DH
    total = k_ref.shape[0]
    columns = group * row_count
    scale = 1.0 / math.sqrt(DH)
    keys = k_ref[...]
    values = v_ref[...]
    key_place = lax.broadcasted_iota(jnp.int32, (total, row_count), 0)
    row_place = ctx_ref[0] * row_count + lax.broadcasted_iota(jnp.int32, (total, row_count), 1)
    visible = jnp.concatenate([jnp.where(key_place <= row_place, 0.0, -jnp.inf)] * group, axis=1)

    def stacked(ref, layer):
        return jnp.concatenate(
            [ref[layer, :, j * DH : (j + 1) * DH] for j in range(group)], axis=0
        )

    def spread(ref, layer, rows):
        for j in range(group):
            ref[layer, :, j * DH : (j + 1) * DH] = rows[j * row_count : (j + 1) * row_count]

    key_grad = jnp.zeros((total, DH), jnp.float32)
    value_grad = jnp.zeros((total, DH), jnp.float32)
    for layer in range(layer_count):
        queries = stacked(q_ref, layer)
        grads = stacked(g_ref, layer)
        scores = lax.dot_general(
            keys, queries, (((1,), (1,)), ((), ())), preferred_element_type=jnp.float32
        )
        scores = scores * scale + visible
        top = jnp.max(scores, axis=0, keepdims=True)
        soft = jnp.exp(scores - top)
        soft = soft * (1.0 / jnp.sum(soft, axis=0, keepdims=True))
        low = soft.astype(jnp.bfloat16)
        mixed = lax.dot_general(
            low, values, (((0,), (0,)), ((), ())), preferred_element_type=jnp.float32
        ).astype(jnp.bfloat16)
        spread(att_ref, layer, mixed)
        product = grads.astype(jnp.float32) * mixed.astype(jnp.float32)
        delta = jnp.sum(product.T, axis=0, keepdims=True)
        prob_grad = lax.dot_general(
            values, grads, (((1,), (1,)), ((), ())), preferred_element_type=jnp.float32
        )
        score_grad = (soft * (prob_grad - delta) * scale).astype(jnp.bfloat16)
        query_grad = lax.dot_general(
            score_grad, keys, (((0,), (0,)), ((), ())), preferred_element_type=jnp.float32
        )
        spread(qg_ref, layer, query_grad.astype(jnp.bfloat16))
        key_grad += jnp.dot(score_grad, queries, preferred_element_type=jnp.float32)
        value_grad += jnp.dot(low, grads, preferred_element_type=jnp.float32)
    kg_ref[...] = key_grad.astype(kg_ref.dtype)
    vg_ref[...] = value_grad.astype(vg_ref.dtype)


def cross_attention(queries, cotangent, full_cache, place):
    layer_count, row_count, model_width = queries.shape
    total, cache_width = full_cache.shape
    kv_heads = cache_width // 2 // DH
    width = model_width // kv_heads
    rows = pl.BlockSpec((layer_count, row_count, width), lambda h, c: (0, 0, h))
    cut = pl.BlockSpec((total, DH), lambda h, c: (0, h))
    cut_values = pl.BlockSpec((total, DH), lambda h, c: (0, kv_heads + h))
    half = jax.ShapeDtypeStruct((total, cache_width // 2), jnp.float32)
    return pl.pallas_call(
        attention_kernel,
        grid_spec=pltpu.PrefetchScalarGridSpec(
            num_scalar_prefetch=1,
            grid=(kv_heads,),
            in_specs=[rows, rows, cut, cut_values],
            out_specs=[rows, rows, cut, cut],
        ),
        out_shape=[
            jax.ShapeDtypeStruct(queries.shape, jnp.bfloat16),
            jax.ShapeDtypeStruct(queries.shape, jnp.bfloat16),
            half,
            half,
        ],
        compiler_params=pltpu.CompilerParams(vmem_limit_bytes=56 * 1024 * 1024),
    )(place, queries, cotangent, full_cache, full_cache)


def body(queries, cotangent, ret_query, ret_key, ret_value, gate_log, kv_weight):
    ret_out = kept_memory_lines(ret_query, ret_key, ret_value, gate_log)
    partial_rows = jnp.dot(ret_out, kv_weight, preferred_element_type=jnp.float32)
    cache = lax.psum(partial_rows, "section").astype(jnp.bfloat16)
    full_cache = lax.all_gather(cache, "ctx", axis=0, tiled=True)
    place = lax.axis_index("ctx").reshape(1)
    attended_all, grad_rows_all, key_grad, value_grad = cross_attention(
        queries, cotangent, full_cache, place
    )
    cache_total = jnp.concatenate([key_grad, value_grad], axis=1)
    own_part = lax.psum_scatter(cache_total, "ctx", scatter_dimension=0, tiled=True)
    summed_grad = lax.psum(own_part, "section")
    cache_grad = summed_grad.astype(jnp.bfloat16)
    retention_grad = jnp.einsum(
        "rw,cw->rc", cache_grad, kv_weight, preferred_element_type=jnp.float32
    ).astype(jnp.bfloat16)
    return (attended_all, grad_rows_all, retention_grad)


def solution(mesh):
    return jax.shard_map(
        body,
        mesh=mesh,
        in_specs=(
            P("section", "ctx", None),
            P("section", "ctx", None),
            P("ctx", "section"),
            P("ctx", "section"),
            P("ctx", "section"),
            P("ctx", "section"),
            P("section", None),
        ),
        out_specs=(P("section", "ctx", None), P("section", "ctx", None), P("ctx", "section")),
        check_vma=False,
    )
```

time: 655 us -> 368 us (0.56); the launches traced: 643 us -> 367 us
  waiting for transfers between devices: 276 us -> 143 us
  local copies, waits for them, and re-layouts: 110 us -> 3.27 us
  Pallas kernels: 0 us -> 57.1 us
  other arithmetic: 57.6 us -> 20.3 us
  matrix products: 39.1 us -> 13 us
  blocking collectives: 142 us -> 117 us
    unnamed x4 -> x3, waiting for transfers between devices: 249 us -> 0.05 us
    reduce_scatter x0 -> x1, waiting for transfers between devices: none -> 81.7 us  [body(): lax.psum_scatter(cache_total, 'ctx', scatter_dimension=0, tiled=True)]
    pallas_call x0 -> x1, Pallas kernels: none -> 57.1 us  [cross_attention(): pl.pallas_call(attention_kernel, grid_spec=pltpu.PrefetchScalarGridSpec(n...]
    another operation x20 -> x2, local copies, waits for them, and re-layouts: 45.8 us -> 0.1 us
    all_gather x1, waiting for transfers between devices: 4.12 us -> 38.8 us  [body(): full_cache = lax.all_gather(cache, 'ctx', axis=0, tiled=True)]
    unnamed x18 -> x5, local copies, waits for them, and re-layouts: 33.3 us -> 0.02 us
    dot_general x14 -> x0, matrix products: 25.8 us -> none  [the longest x4 11.4 us: block_scores(): jnp.einsum('rkgd,ukd->kgru', query_heads, key_block, preferred_element_ty...]
    psum x1, blocking collectives: 78.1 us -> 52.7 us  [body(): summed_grad = lax.psum(own_part, 'section')]
  transfers between devices with their start and end apart: 3 -> 3, of which waited for: 3 -> 3; matrix products, arithmetic and copies ran while one was open for 10% -> 1% of each run, Pallas kernels for 0% -> 0%
where the time goes in v1:
time: 368 us; the launch traced here: 367 us
  waiting for transfers between devices  143 us (39%)
  blocking collectives  117 us (32%)
  Pallas kernels  57.1 us (16%)
  other arithmetic  20.3 us (6%)
  between operations  13.8 us (4%)
  matrix products  13 us (4%)
    reduce_scatter x1, waiting for transfers between devices, body(): lax.psum_scatter(cache_total, 'ctx', scatter_dimension=0, tiled=True)  81.7 us
    pallas_call x1, Pallas kernels, cross_attention(): pl.pallas_call(attention_kernel, grid_spec=pltpu.PrefetchScalarGridSpec(n...  57.1 us
    psum x1, blocking collectives, body(): cache = lax.psum(partial_rows, 'section').astype(jnp.bfloat16)  53.5 us
    psum x1, blocking collectives, body(): summed_grad = lax.psum(own_part, 'section')  52.7 us
    all_gather x1, waiting for transfers between devices, body(): full_cache = lax.all_gather(cache, 'ctx', axis=0, tiled=True)  38.8 us
    all_gather x1, waiting for transfers between devices, entering(): pieces = jax.tree.map(lambda part: lax.all_gather(part, axis), value)  22.4 us
    all_gather x1, blocking collectives, entering(): pieces = jax.tree.map(lambda part: lax.all_gather(part, axis), value)  10.3 us
    concatenate x1, other arithmetic, body(): cache_total = jnp.concatenate([key_grad, value_grad], axis=1)  9.69 us
  transfers between devices with their start and end apart: 3, of which 3 were waited for; matrix products, arithmetic and copies ran while one was open for 1% of the time, Pallas kernels for 0%

profile of v1, /device:TPU:0, one launch (start us, length us, event | category | flops | bytes accessed | tf_op | source)
XLA Modules:
  0.0 367.4 jit_solution(5776163120916538647)
XLA Ops:
  8.1 1.8 reduce-window.6
  11.7 1.2 reshape.59
  13.2 2.6 fusion.4
  15.9 10.3 %all-gather.1 = f32[8,1,6]{2,1,0:T(1,128)S(1)} all-gather(f32[1,1,6]{2,1,0:T(1,128)} %bitcast.85), channel_id=1, replica_groups=mesh['section'=4,'ctx'=8] {'ctx'}, dimensions={0}, use_global_device_ids=true | all-gather | bytes 216 | tf_op jit(solution)/shard_map/all_gather | solution.py:19
  26.2 2.4 convolution_multiply_fusion
  28.6 22.4 %all-gather.7.cloned.1.call-done = f32[48,128,128]{2,1,0:T(8,128)} async-done(((f32[6,128,128]{2,1,0:T(8,128)}), f32[48,128,128]{2,1,0:T(8,128)}) %all-gather.7.cloned.1.call-update) | async-done | bytes 3145744 | tf_op jit(solution)/shard_map/all_gather | solution.py:19
  51.0 8.1 %while.14 = (s32[]{:T(128)}, f32[6,128,128]{2,1,0:T(8,128)S(1)}, s32[]{:T(128)}, f32[8,6]{1,0:T(8,128)S(1)}, f32[8,6,128,128]{3,2,1,0:T(8,128)}, /*index=5*/s32[]{:T(128)}, s32[]{:T(128)}) while((s32[]{:T(128)}, f32[6,128,128]{2,1,0:T(8,128)S(1)}, s32[]{:T(128)}, f32[8,6]{1,0:T(8,128)S(1)}, f32[8,6,128,128]{3,2,1,0:T(8,128)}, ...), condition=%wide.region_3.4_spmd.clone, body=%wide.region_2.3_spmd.clone.sunk | while | flops 393220 | bytes 1179833 | solution.py:28
  51.0 1.1 fusion.33
  52.1 1.1 fusion.33
  53.3 1.1 fusion.33
  54.5 1.1 fusion.33
  55.6 1.1 fusion.33
  56.8 1.1 fusion.33
  57.9 1.1 fusion.33
  59.1 1.3 fusion.2
  60.4 2.0 multiply_reduce_fusion
  62.4 1.8 fusion.7
  64.2 53.5 %all-reduce.3 = bf16[160,2048]{1,0:T(8,128)(2,1)} all-reduce(f32[160,2048]{1,0:T(8,128)} %fusion.7), channel_id=1, replica_groups=mesh['section'=4,'ctx'=8] {'section'}, use_global_device_ids=true, to_apply=%region_5.6 | all-reduce | flops 327680 | bytes 1966080 | tf_op jit(solution)/shard_map/psum | solution.py:146
  117.8 38.8 %all-gather.5.cloned.1.call-done.k_ref.v_ref = bf16[1280,2048]{1,0:T(8,128)(2,1)} async-done(((bf16[160,2048]{1,0:T(8,128)(2,1)}), bf16[1280,2048]{1,0:T(8,128)(2,1)}) %all-gather.5.cloned.1.call-update) | async-done | bytes 5242896 | tf_op jit(solution)/shard_map/all_gather | solution.py:147
  156.6 57.1 %shard_map.94 = (bf16[2,160,3072]{2,1,0:T(8,128)(2,1)}, bf16[2,160,3072]{2,1,0:T(8,128)(2,1)}, f32[1280,1024]{1,0:T(8,128)}, f32[1280,1024]{1,0:T(8,128)}) custom-call(s32[1]{0:T(128)} %bitcast.ctx_ref, bf16[2,160,3072]{2,1,0:T(8,128)(2,1)} %q_ref.1, bf16[2,160,3072]{2,1,0:T(8,128)(2,1)} %g_ref.1, ...), custom_call_target="tpu_custom_call" | custom-call | tf_op jit(solution)/shard_map/pallas_call | solution.py:125
  213.8 9.7 %pad_maximum_fusion = f32[1280,2048]{1,0:T(8,128)} fusion(f32[1280,1024]{1,0:T(8,128)} %get-tuple-element.105, f32[1280,1024]{1,0:T(8,128)} %get-tuple-element.104), kind=kLoop, calls=%fused_computation.3 | loop fusion | flops 2621440 | bytes 20971520 | tf_op jit(solution)/shard_map/concatenate | solution.py:152
  223.5 81.7 %reduce-scatter.2.cloned.1.call-done = f32[160,2048]{1,0:T(8,128)} async-done(((f32[1280,2048]{1,0:T(8,128)}), f32[160,2048]{1,0:T(8,128)}) %reduce-scatter.2.cloned.1.call-update) | async-done | bytes 1310736 | tf_op jit(solution)/shard_map/reduce_scatter | solution.py:153
  305.2 52.7 %all-reduce.4 = bf16[160,2048]{1,0:T(8,128)(2,1)} all-reduce(f32[160,2048]{1,0:T(8,128)} %reduce-scatter.2.cloned.1.call-done), channel_id=1, replica_groups=mesh['section'=4,'ctx'=8] {'section'}, use_global_device_ids=true, to_apply=%region_7.8 | all-reduce | flops 327680 | bytes 1966080 | tf_op jit(solution)/shard_map/psum | solution.py:154
  357.9 3.0 convolution_convert_fusion
  (33 shorter events, 3.2 us)
Async XLA Ops:
  7.2 55.2 %copy-start = (bf16[768,2048]{1,0:T(8,128)(2,1)S(1)}, bf16[768,2048]{1,0:T(8,128)(2,1)}, u32[]{:S(2)}) copy-start(bf16[768,2048]{1,0:T(8,128)(2,1)} %param.15) | copy-start | bytes 9437188
  7.2 43.8 %all-gather.7.cloned.1.call-start = ((), (), s32[]{:S(2)}) async-start(), calls=%async_computation.3 | async-start | bytes 3538944 | tf_op jit(solution)/shard_map/all_gather | solution.py:19
  15.8 140.8 %all-gather.5.cloned.1.call-start = ((), (), s32[]{:S(2)}) async-start(), calls=%async_computation.1 | async-start | bytes 5898240 | tf_op jit(solution)/shard_map/all_gather | solution.py:147
  28.6 30.5 %copy-start.1 = (f32[160,6]{0,1:T(8,128)S(1)}, f32[160,6]{0,1:T(8,128)}, u32[]{:S(2)}) copy-start(f32[160,6]{0,1:T(8,128)} %get-tuple-element.137) | copy-start | bytes 11524
  117.8 187.4 %reduce-scatter.2.cloned.1.call-start = ((), (), s32[]{:S(2)}) async-start(), calls=%async_computation.2 | async-start | bytes 11796480 | tf_op jit(solution)/shard_map/reduce_scatter | solution.py:153
Sparse Core Ops, SparseCore 0:
  15.9 35.0 all-gather.6
  117.9 38.6 all-gather.4
  223.6 81.5 reduce-scatter.1

commit v2 on v1

v2 whole, which is shorter than its diff:
```python
import functools
import math

import jax
import jax.numpy as jnp
from jax import lax
from jax.experimental import pallas as pl
from jax.experimental.pallas import tpu as pltpu
from jax.sharding import PartitionSpec as P

DH = 128


epsilon = 1e-06
highest = lax.Precision.HIGHEST

MESH = pl.DeviceIdType.MESH
LIMIT = 56 * 1024 * 1024


def greet(peers):
    barrier = pltpu.get_barrier_semaphore()
    for peer in peers:
        pl.semaphore_signal(barrier, inc=1, device_id=peer, device_id_type=MESH)
    pl.semaphore_wait(barrier, len(peers))


def remote(source, target, send_sem, recv_sem, device):
    return pltpu.make_async_remote_copy(
        src_ref=source,
        dst_ref=target,
        send_sem=send_sem,
        recv_sem=recv_sem,
        device_id=device,
        device_id_type=MESH,
    )


def two_part_dot(wide, narrow, dims):
    high = wide.astype(jnp.bfloat16)
    low = (wide - high.astype(jnp.float32)).astype(jnp.bfloat16)
    return lax.dot_general(
        high, narrow, dims, preferred_element_type=jnp.float32
    ) + lax.dot_general(low, narrow, dims, preferred_element_type=jnp.float32)


def cache_kernel(
    n_sec,
    n_ctx,
    q_ref,
    k_ref,
    v_ref,
    gate_ref,
    turned_ref,
    w_ref,
    out_ref,
    ret,
    raw,
    own_state,
    own_total,
    sib_state,
    sib_total,
    chip_state,
    chip_total,
    got_state,
    got_total,
    running,
    send_part,
    got_part,
    sib_send,
    sib_recv,
    st_send,
    st_recv,
    tot_send,
    tot_recv,
    part_send,
    part_recv,
    z_send,
    z_recv,
    x_send,
    x_recv,
    y_send,
    y_recv,
):
    sec, ctx = lax.axis_index("section"), lax.axis_index("ctx")
    chip, core = lax.div(ctx, 2), lax.rem(ctx, 2)
    n_chip = n_ctx // 2
    sibling = (sec, chip * 2 + 1 - core)
    rows, width = q_ref.shape
    heads = width // DH
    columns = out_ref.shape[1]
    piece = columns // n_sec
    half = columns // 2
    row_dims = (((0,), (0,)), ((), ()))
    plain = (((1,), (0,)), ((), ()))
    last_dims = (((1,), (1,)), ((), ()))

    greet(
        [(lax.rem(sec + j, n_sec), ctx) for j in range(1, n_sec)]
        + [(sec, lax.rem(ctx + j, n_ctx)) for j in range(1, n_ctx)]
    )

    first = lax.broadcasted_iota(jnp.int32, (rows, rows), 0)
    second = lax.broadcasted_iota(jnp.int32, (rows, rows), 1)
    causal = first >= second
    cumulative = jnp.dot(
        causal.astype(jnp.float32), gate_ref[...], precision=highest,
        preferred_element_type=jnp.float32,
    )
    turned = jnp.dot(
        turned_ref[...], (first <= second).astype(jnp.float32), precision=highest,
        preferred_element_type=jnp.float32,
    )
    total = cumulative[rows - 1 : rows]
    own_total[...] = jnp.broadcast_to(total, own_total.shape)
    tail = jnp.exp(total - cumulative)
    for h in range(heads):
        cut = slice(h * DH, (h + 1) * DH)
        decayed = k_ref[:, cut].astype(jnp.float32) * tail[:, h : h + 1]
        own_state[h] = two_part_dot(decayed, v_ref[:, cut], row_dims).astype(jnp.bfloat16)

    def to_sibling(index):
        pair = ((own_state, sib_state), (own_total, sib_total))[index]
        return remote(*pair, sib_send.at[index], sib_recv.at[index], sibling)

    @pl.when(core == 0)
    def _():
        to_sibling(0).start()
        to_sibling(1).start()

    def chip_copy(r, c, index):
        if index == 0:
            return remote(
                chip_state, got_state.at[chip], st_send.at[r, c], st_recv.at[chip], (sec, 2 * r + c)
            )
        return remote(
            chip_total, got_total.at[chip], tot_send.at[r, c], tot_recv.at[chip], (sec, 2 * r + c)
        )

    @pl.when(core == 1)
    def _():
        to_sibling(0).wait_recv()
        to_sibling(1).wait_recv()
        chip_total[...] = own_total[...] + sib_total[...]
        kept = jnp.exp(total)
        for h in range(heads):
            chip_state[h] = (
                sib_state[h].astype(jnp.float32) * kept[:, h : h + 1]
                + own_state[h].astype(jnp.float32)
            ).astype(jnp.bfloat16)
        for r in range(n_chip - 1, 0, -1):

            @pl.when(chip < r)
            def _():
                for c in range(2):
                    chip_copy(r, c, 1).start()
                    chip_copy(r, c, 0).start()

    for h in range(heads):
        cut = slice(h * DH, (h + 1) * DH)
        spread = cumulative[:, h : h + 1] - turned[h : h + 1, :]
        weights = jnp.exp(jnp.where(causal, spread, -jnp.inf))
        scores = lax.dot_general(
            q_ref[:, cut], k_ref[:, cut], last_dims, preferred_element_type=jnp.float32
        )
        raw[:, cut] = two_part_dot(weights * scores, v_ref[:, cut], plain)

    running[...] = jnp.zeros_like(running)
    for r in range(n_chip - 1):

        @pl.when(r < chip)
        def _():
            remote(
                chip_total, got_total.at[r], tot_send.at[r, 0], tot_recv.at[r], sibling
            ).wait_recv()
            remote(
                chip_state, got_state.at[r], st_send.at[r, 0], st_recv.at[r], sibling
            ).wait_recv()
            kept = jnp.exp(got_total[r][0:1])
            for h in range(heads):
                running[h] = running[h] * kept[:, h : h + 1] + got_state[r, h].astype(jnp.float32)

    @pl.when(core == 1)
    def _():
        kept = jnp.exp(sib_total[0:1])
        for h in range(heads):
            running[h] = running[h] * kept[:, h : h + 1] + sib_state[h].astype(jnp.float32)

    grown = jnp.exp(cumulative)
    for h in range(heads):
        cut = slice(h * DH, (h + 1) * DH)
        state = running[h]
        high = state.astype(jnp.bfloat16)
        low = (state - high.astype(jnp.float32)).astype(jnp.bfloat16)
        carried = jnp.dot(q_ref[:, cut], high, preferred_element_type=jnp.float32) + jnp.dot(
            q_ref[:, cut], low, preferred_element_type=jnp.float32
        )
        whole = raw[:, cut] + grown[:, h : h + 1] * carried
        square = jnp.mean(whole * whole, axis=1, keepdims=True)
        ret[:, cut] = (whole * lax.rsqrt(square + epsilon)).astype(jnp.bfloat16)

    def part_of(s):
        start = pl.multiple_of(s * piece, piece)
        return jnp.dot(ret[...], w_ref[:, pl.ds(start, piece)], preferred_element_type=jnp.float32)

    def part_copy(j):
        return remote(
            send_part.at[j - 1], got_part.at[j - 1], part_send.at[j - 1], part_recv.at[j - 1],
            (lax.rem(sec + j, n_sec), ctx),
        )

    for j in range(1, n_sec):
        send_part[j - 1] = part_of(lax.rem(sec + j, n_sec)).astype(jnp.bfloat16)
        part_copy(j).start()
    summed = part_of(sec)
    for r in range(1, n_ctx):

        @pl.when(r > ctx)
        def _():
            out_ref[r * rows : (r + 1) * rows, :] = jnp.zeros((rows, columns), jnp.bfloat16)

    for j in range(1, n_sec):
        part_copy(j).wait_recv()
        summed += got_part[j - 1].astype(jnp.float32)
    my_rows = pl.ds(pl.multiple_of(ctx * rows, rows), rows)
    my_cut = pl.ds(pl.multiple_of(sec * piece, piece), piece)
    out_ref[my_rows, my_cut] = summed.astype(jnp.bfloat16)

    def z_copy(j):
        spot = out_ref.at[my_rows, my_cut]
        return remote(spot, spot, z_send.at[j - 1], z_recv.at[j - 1], (lax.rem(sec + j, n_sec), ctx))

    for j in range(1, n_sec):
        z_copy(j).start()
    for j in range(1, n_sec):
        z_copy(j).wait_recv()

    def x_copy(r, c):
        spot = out_ref.at[my_rows, c * half : (c + 1) * half]
        return remote(spot, spot, x_send.at[r, c], x_recv.at[ctx], (sec, 2 * r + c))

    def y_copy(d, c, cut, device):
        spot = out_ref.at[d * rows : (d + 1) * rows, cut]
        return remote(spot, spot, y_send.at[d], y_recv.at[d], device)

    for r in range(n_chip - 1, 0, -1):

        @pl.when(r > chip)
        def _():
            for c in range(2):
                x_copy(r, c).start()

    def own_copy():
        spot = out_ref.at[my_rows, :]
        return remote(spot, spot, y_send.at[n_ctx], y_recv.at[n_ctx], sibling)

    @pl.when(core == 0)
    def _():
        own_copy().start()

    my_half = pl.ds(pl.multiple_of(core * half, half), half)
    for d in range(n_ctx - 3, -1, -1):

        @pl.when(d < chip * 2)
        def _():
            spot = out_ref.at[d * rows : (d + 1) * rows, my_half]
            remote(spot, spot, x_send.at[0, 0], x_recv.at[d], sibling).wait_recv()
            y_copy(d, core, my_half, sibling).start()

    other_half = pl.ds(pl.multiple_of((1 - core) * half, half), half)
    for d in range(n_ctx - 2):

        @pl.when(d < chip * 2)
        def _():
            y_copy(d, core, other_half, sibling).wait_recv()
            y_copy(d, core, my_half, sibling).wait_send()

    @pl.when(core == 0)
    def _():
        own_copy().wait_send()
        to_sibling(0).wait_send()
        to_sibling(1).wait_send()

    @pl.when(core == 1)
    def _():
        spot = out_ref.at[pl.ds(pl.multiple_of((ctx - core) * rows, rows), rows), :]
        remote(spot, spot, y_send.at[n_ctx], y_recv.at[n_ctx], sibling).wait_recv()

    for r in range(1, n_chip):

        @pl.when(r > chip)
        def _():
            for c in range(2):
                x_copy(r, c).wait_send()

            @pl.when(core == 1)
            def _():
                for c in range(2):
                    chip_copy(r, c, 0).wait_send()
                    chip_copy(r, c, 1).wait_send()

    for j in range(1, n_sec):
        part_copy(j).wait_send()
        z_copy(j).wait_send()


def shared_cache(ret_query, ret_key, ret_value, gate_log, kv_weight):
    n_sec, n_ctx = lax.axis_size("section"), lax.axis_size("ctx")
    n_chip = n_ctx // 2
    rows, width = ret_query.shape
    heads = width // DH
    columns = kv_weight.shape[1]
    piece = columns // n_sec
    gate = jnp.pad(gate_log, ((0, 0), (0, 128 - heads)))
    turned = jnp.pad(gate_log.T, ((0, 8 - heads), (0, 0)))
    state = pltpu.VMEM((heads, DH, DH), jnp.bfloat16)
    total = pltpu.VMEM((8, 128), jnp.float32)
    dma = pltpu.SemaphoreType.DMA
    vmem = pl.BlockSpec(memory_space=pltpu.VMEM)
    return pl.pallas_call(
        functools.partial(cache_kernel, n_sec, n_ctx),
        out_shape=jax.ShapeDtypeStruct((n_ctx * rows, columns), jnp.bfloat16),
        in_specs=[vmem] * 6,
        out_specs=vmem,
        scratch_shapes=[
            pltpu.VMEM((rows, width), jnp.bfloat16),
            pltpu.VMEM((rows, width), jnp.float32),
            state, total, state, total, state, total,
            pltpu.VMEM((n_chip, heads, DH, DH), jnp.bfloat16),
            pltpu.VMEM((n_chip, 8, 128), jnp.float32),
            pltpu.VMEM((heads, DH, DH), jnp.float32),
            pltpu.VMEM((n_sec - 1, rows, piece), jnp.bfloat16),
            pltpu.VMEM((n_sec - 1, rows, piece), jnp.bfloat16),
            dma((2,)), dma((2,)),
            dma((n_chip, 2)), dma((n_chip,)),
            dma((n_chip, 2)), dma((n_chip,)),
            dma((n_sec - 1,)), dma((n_sec - 1,)),
            dma((n_sec - 1,)), dma((n_sec - 1,)),
            dma((n_chip, 2)), dma((n_ctx,)),
            dma((n_ctx + 1,)), dma((n_ctx + 1,)),
        ],
        compiler_params=pltpu.CompilerParams(
            collective_id=0, has_side_effects=True, vmem_limit_bytes=LIMIT
        ),
    )(ret_query, ret_key, ret_value, gate, turned, kv_weight)


def gradient_kernel(
    n_sec,
    n_ctx,
    kg_ref,
    vg_ref,
    out_ref,
    from_sib,
    send_chip,
    got_chip,
    kept,
    send_part,
    got_part,
    final,
    sib_send,
    sib_recv,
    chip_send,
    chip_recv,
    part_send,
    part_recv,
    all_send,
    all_recv,
):
    sec, ctx = lax.axis_index("section"), lax.axis_index("ctx")
    chip, core = lax.div(ctx, 2), lax.rem(ctx, 2)
    n_chip = n_ctx // 2
    sibling = (sec, chip * 2 + 1 - core)
    rows = out_ref.shape[0]
    pair = 2 * rows
    half = kg_ref.shape[1]
    piece = half // n_sec

    others = [(lax.rem(sec + j, n_sec), chip * 2 + lax.rem(core + c, 2), j, c)
              for j in range(n_sec) for c in range(2) if j or c]
    greet(
        [(s, d) for s, d, _, _ in others]
        + [(sec, lax.rem(ctx + 2 * i, n_ctx)) for i in range(1, n_chip)]
    )

    def sib_copy(r, ref):
        return remote(
            ref.at[r * pair : (r + 1) * pair, :], from_sib.at[r], sib_send.at[r], sib_recv.at[r],
            sibling,
        )

    for r in range(n_chip):

        @pl.when(jnp.logical_and(r <= chip, core == 0))
        def _():
            sib_copy(r, vg_ref).start()

        @pl.when(jnp.logical_and(r <= chip, core == 1))
        def _():
            sib_copy(r, kg_ref).start()

    def chip_copy(r):
        return remote(
            send_chip.at[r], got_chip.at[chip], chip_send.at[r], chip_recv.at[chip],
            (sec, 2 * r + core),
        )

    for r in range(n_chip):

        @pl.when(r <= chip)
        def _():
            sib_copy(r, kg_ref).wait_recv()
            cut = slice(r * pair, (r + 1) * pair)

            @pl.when(core == 0)
            def _():
                kept[...] = kg_ref[cut, :].astype(jnp.float32) + from_sib[r].astype(jnp.float32)

            @pl.when(core == 1)
            def _():
                kept[...] = vg_ref[cut, :].astype(jnp.float32) + from_sib[r].astype(jnp.float32)

            @pl.when(r < chip)
            def _():
                send_chip[r] = kept[...].astype(jnp.bfloat16)
                chip_copy(r).start()

    for r in range(1, n_chip):

        @pl.when(r > chip)
        def _():
            remote(
                send_chip.at[r], got_chip.at[r], chip_send.at[r], chip_recv.at[r], sibling
            ).wait_recv()
            kept[...] += got_chip[r].astype(jnp.float32)

    def part_copy(j):
        return remote(
            send_part.at[j - 1], got_part.at[j - 1], part_send.at[j - 1], part_recv.at[j - 1],
            (lax.rem(sec + j, n_sec), ctx),
        )

    def cut_of(s):
        return pl.ds(pl.multiple_of(s * piece, piece), piece)

    for j in range(1, n_sec):
        send_part[j - 1] = kept[:, cut_of(lax.rem(sec + j, n_sec))].astype(jnp.bfloat16)
        part_copy(j).start()
    summed = kept[:, cut_of(sec)]
    for j in range(1, n_sec):
        part_copy(j).wait_recv()
        summed += got_part[j - 1].astype(jnp.float32)
    final[...] = summed.astype(jnp.bfloat16)
    place = pl.ds(pl.multiple_of(core * half + sec * piece, piece), piece)

    def all_copy(s, d, j, c):
        part = pl.ds(pl.multiple_of(lax.rem(core + c, 2) * rows, rows), rows)
        return remote(
            final.at[part, :], out_ref.at[:, place], all_send.at[j, c], all_recv.at[j, c], (s, d)
        )

    for s, d, j, c in others:
        all_copy(s, d, j, c).start()
    out_ref[:, place] = final[pl.ds(pl.multiple_of(core * rows, rows), rows), :]
    for s, d, j, c in others:
        all_copy(s, d, j, c).wait_recv()
    for s, d, j, c in others:
        all_copy(s, d, j, c).wait_send()
    for j in range(1, n_sec):
        part_copy(j).wait_send()
    for r in range(n_chip):

        @pl.when(r <= chip)
        def _():
            sib_copy(r, kg_ref).wait_send()

        @pl.when(r < chip)
        def _():
            chip_copy(r).wait_send()


def summed_gradient(key_grad, value_grad):
    n_sec, n_ctx = lax.axis_size("section"), lax.axis_size("ctx")
    n_chip = n_ctx // 2
    total, half = key_grad.shape
    rows = total // n_ctx
    pair = 2 * rows
    piece = half // n_sec
    dma = pltpu.SemaphoreType.DMA
    vmem = pl.BlockSpec(memory_space=pltpu.VMEM)
    chips = pltpu.VMEM((n_chip, pair, half), jnp.bfloat16)
    parts = pltpu.VMEM((n_sec - 1, pair, piece), jnp.bfloat16)
    return pl.pallas_call(
        functools.partial(gradient_kernel, n_sec, n_ctx),
        out_shape=jax.ShapeDtypeStruct((rows, 2 * half), jnp.bfloat16),
        in_specs=[vmem] * 2,
        out_specs=vmem,
        scratch_shapes=[
            chips, chips, chips,
            pltpu.VMEM((pair, half), jnp.float32),
            parts, parts,
            pltpu.VMEM((pair, piece), jnp.bfloat16),
            dma((n_chip,)), dma((n_chip,)),
            dma((n_chip,)), dma((n_chip,)),
            dma((n_sec - 1,)), dma((n_sec - 1,)),
            dma((n_sec, 2)), dma((n_sec, 2)),
        ],
        compiler_params=pltpu.CompilerParams(
            collective_id=1, has_side_effects=True, vmem_limit_bytes=LIMIT
        ),
    )(key_grad, value_grad)


def attention_kernel(ctx_ref, q_ref, g_ref, k_ref, v_ref, att_ref, qg_ref, kg_ref, vg_ref):
    layer_count, row_count, width = q_ref.shape
    group = width // DH
    total = k_ref.shape[0]
    columns = group * row_count
    scale = 1.0 / math.sqrt(DH)
    keys = k_ref[...]
    values = v_ref[...]
    key_place = lax.broadcasted_iota(jnp.int32, (total, row_count), 0)
    row_place = ctx_ref[0] * row_count + lax.broadcasted_iota(jnp.int32, (total, row_count), 1)
    visible = jnp.concatenate([jnp.where(key_place <= row_place, 0.0, -jnp.inf)] * group, axis=1)

    def stacked(ref, layer):
        return jnp.concatenate(
            [ref[layer, :, j * DH : (j + 1) * DH] for j in range(group)], axis=0
        )

    def spread(ref, layer, rows):
        for j in range(group):
            ref[layer, :, j * DH : (j + 1) * DH] = rows[j * row_count : (j + 1) * row_count]

    key_grad = jnp.zeros((total, DH), jnp.float32)
    value_grad = jnp.zeros((total, DH), jnp.float32)
    for layer in range(layer_count):
        queries = stacked(q_ref, layer)
        grads = stacked(g_ref, layer)
        scores = lax.dot_general(
            keys, queries, (((1,), (1,)), ((), ())), preferred_element_type=jnp.float32
        )
        scores = scores * scale + visible
        top = jnp.max(scores, axis=0, keepdims=True)
        soft = jnp.exp(scores - top)
        soft = soft * (1.0 / jnp.sum(soft, axis=0, keepdims=True))
        low = soft.astype(jnp.bfloat16)
        mixed = lax.dot_general(
            low, values, (((0,), (0,)), ((), ())), preferred_element_type=jnp.float32
        ).astype(jnp.bfloat16)
        spread(att_ref, layer, mixed)
        product = grads.astype(jnp.float32) * mixed.astype(jnp.float32)
        delta = jnp.sum(product.T, axis=0, keepdims=True)
        prob_grad = lax.dot_general(
            values, grads, (((1,), (1,)), ((), ())), preferred_element_type=jnp.float32
        )
        score_grad = (soft * (prob_grad - delta) * scale).astype(jnp.bfloat16)
        query_grad = lax.dot_general(
            score_grad, keys, (((0,), (0,)), ((), ())), preferred_element_type=jnp.float32
        )
        spread(qg_ref, layer, query_grad.astype(jnp.bfloat16))
        key_grad += jnp.dot(score_grad, queries, preferred_element_type=jnp.float32)
        value_grad += jnp.dot(low, grads, preferred_element_type=jnp.float32)
    kg_ref[...] = key_grad.astype(kg_ref.dtype)
    vg_ref[...] = value_grad.astype(vg_ref.dtype)


def cross_attention(queries, cotangent, full_cache, place):
    layer_count, row_count, model_width = queries.shape
    total, cache_width = full_cache.shape
    kv_heads = cache_width // 2 // DH
    width = model_width // kv_heads
    rows = pl.BlockSpec((layer_count, row_count, width), lambda h, c: (0, 0, h))
    cut = pl.BlockSpec((total, DH), lambda h, c: (0, h))
    cut_values = pl.BlockSpec((total, DH), lambda h, c: (0, kv_heads + h))
    half = jax.ShapeDtypeStruct((total, cache_width // 2), jnp.bfloat16)
    return pl.pallas_call(
        attention_kernel,
        grid_spec=pltpu.PrefetchScalarGridSpec(
            num_scalar_prefetch=1,
            grid=(kv_heads,),
            in_specs=[rows, rows, cut, cut_values],
            out_specs=[rows, rows, cut, cut],
        ),
        out_shape=[
            jax.ShapeDtypeStruct(queries.shape, jnp.bfloat16),
            jax.ShapeDtypeStruct(queries.shape, jnp.bfloat16),
            half,
            half,
        ],
        compiler_params=pltpu.CompilerParams(vmem_limit_bytes=LIMIT),
    )(place, queries, cotangent, full_cache, full_cache)


def body(queries, cotangent, ret_query, ret_key, ret_value, gate_log, kv_weight):
    full_cache = shared_cache(ret_query, ret_key, ret_value, gate_log, kv_weight)
    place = lax.axis_index("ctx").reshape(1)
    attended_all, grad_rows_all, key_grad, value_grad = cross_attention(
        queries, cotangent, full_cache, place
    )
    cache_grad = summed_gradient(key_grad, value_grad)
    retention_grad = jnp.einsum(
        "rw,cw->rc", cache_grad, kv_weight, preferred_element_type=jnp.float32
    ).astype(jnp.bfloat16)
    return (attended_all, grad_rows_all, retention_grad)


def solution(mesh):
    return jax.shard_map(
        body,
        mesh=mesh,
        in_specs=(
            P("section", "ctx", None),
            P("section", "ctx", None),
            P("ctx", "section"),
            P("ctx", "section"),
            P("ctx", "section"),
            P("ctx", "section"),
            P("section", None),
        ),
        out_specs=(P("section", "ctx", None), P("section", "ctx", None), P("ctx", "section")),
        check_vma=False,
    )
```

time: 368 us -> 208 us (0.57)
  waiting for transfers between devices: 143 us -> 0 us
  Pallas kernels: 57.1 us -> 198 us
  blocking collectives: 117 us -> 0 us
  other arithmetic: 20.3 us -> 0 us
  between operations: 13.8 us -> 0.67 us
  matrix products: 13 us -> 2.97 us
    pallas_call x0 -> x2, Pallas kernels: none -> 141 us  [the longest x1 72.2 us: summed_gradient(): pl.pallas_call(functools.partial(gradient_kernel, n_sec, n_ctx), out_shap...]
    psum x2 -> x0, blocking collectives: 106 us -> none  [the longest x1 53.5 us: body(): cache = lax.psum(partial_rows, 'section').astype(jnp.bfloat16)]
    reduce_scatter x1 -> x0, waiting for transfers between devices: 81.7 us -> none  [body(): lax.psum_scatter(cache_total, 'ctx', scatter_dimension=0, tiled=True)]
    all_gather x2 -> x0, waiting for transfers between devices: 61.2 us -> none  [the longest x1 38.8 us: body(): full_cache = lax.all_gather(cache, 'ctx', axis=0, tiled=True)]
    all_gather x1 -> x0, blocking collectives: 10.3 us -> none  [entering(): pieces = jax.tree.map(lambda part: lax.all_gather(part, axis), value)]
    dot_general x5 -> x0, matrix products: 10.1 us -> none  [the longest x1 2.56 us: kept_memory_lines(): jnp.einsum('uh,uhd,uhe->hde', tail_decay, key_part, value_part, precision...]
    concatenate x1 -> x0, other arithmetic: 9.69 us -> none  [body(): cache_total = jnp.concatenate([key_grad, value_grad], axis=1)]
    select_n x7 -> x0, other arithmetic: 7.81 us -> none  [lap(): jnp.where(position < mine, new, old)]
  transfers between devices with their start and end apart: 3 -> 0, of which waited for: 3 -> 0; matrix products, arithmetic and copies ran while one was open for 1% -> 0% of each run, Pallas kernels for 0% -> 0%
where the time goes in v2:
time: 208 us; the launch traced here: 205 us
  Pallas kernels  198 us (95%)
  matrix products  2.97 us (1%)
  local copies, waits for them, and re-layouts  2.75 us (1%)
    pallas_call x1, Pallas kernels, summed_gradient(): pl.pallas_call(functools.partial(gradient_kernel, n_sec, n_ctx), out_shap...  72.2 us
    pallas_call x1, Pallas kernels, shared_cache(): pl.pallas_call(functools.partial(cache_kernel, n_sec, n_ctx), out_shape=j...  69.2 us
    pallas_call x1, Pallas kernels, cross_attention(): pl.pallas_call(attention_kernel, grid_spec=pltpu.PrefetchScalarGridSpec(n...  57.1 us

profile of v2, /device:TPU:0, one launch (start us, length us, event | category | flops | bytes accessed | tf_op | source)
XLA Modules:
  0.0 204.9 jit_solution(16395806283164331382)
XLA Ops:
  0.6 1.3 pad.9.turned_ref
  1.9 0.8 copy.10
  2.7 0.6 pad.8.gate_ref
  3.4 69.2 %shard_map.94.k_ref.v_ref = bf16[1280,2048]{1,0:T(8,128)(2,1)} custom-call(bf16[160,768]{1,0:T(8,128)(2,1)} %q_ref.2, bf16[160,768]{1,0:T(8,128)(2,1)} %k_ref.1, bf16[160,768]{1,0:T(8,128)(2,1)} %v_ref.1, f32[160,128]{1,0:T(8,128)} %pad.8.gate_ref, f32[8,160]{1,0:T(8,128)} %pad.9.turned_ref, bf16[768,2048]{1,0:T(8,128)(2,1)} %w_ref.1), custom_call_target="tpu_custom_call" | custom-call | tf_op jit(solution)/shard_map/pallas_call | solution.py:320
  72.6 57.1 %shard_map.95 = (bf16[2,160,3072]{2,1,0:T(8,128)(2,1)}, bf16[2,160,3072]{2,1,0:T(8,128)(2,1)}, bf16[1280,1024]{1,0:T(8,128)(2,1)}, bf16[1280,1024]{1,0:T(8,128)(2,1)}) custom-call(s32[1]{0:T(128)} %bitcast.ctx_ref, bf16[2,160,3072]{2,1,0:T(8,128)(2,1)} %q_ref.3, bf16[2,160,3072]{2,1,0:T(8,128)(2,1)} %g_ref.1, bf16[1280,2048]{1,0:T(8,128)(2,1)} %shard_map.94.k_ref.v_ref, ...), custom_call_target="tpu_custom_call" | custom-call | tf_op jit(solution)/shard_map/pallas_call | solution.py:577
  129.6 0.0 copy-start
  129.6 72.2 %shard_map.96 = bf16[160,2048]{1,0:T(8,128)(2,1)} custom-call(bf16[1280,1024]{1,0:T(8,128)(2,1)} %get-tuple-element.9.kg_ref, bf16[1280,1024]{1,0:T(8,128)(2,1)} %get-tuple-element.10.vg_ref), custom_call_target="tpu_custom_call" | custom-call | tf_op jit(solution)/shard_map/pallas_call | solution.py:493
  201.9 0.0 copy-done
  201.9 3.0 %convolution_convert_fusion = bf16[160,768]{1,0:T(8,128)(2,1)} fusion(bf16[160,2048]{1,0:T(8,128)(2,1)} %shard_map.96, bf16[768,2048]{1,0:T(8,128)(2,1)S(1)} %copy-done), kind=kOutput, calls=%fused_computation | convolution fusion | flops 503439360 | bytes 4046848 | tf_op jit(solution)/shard_map/rw,cw->rc/dot_general | solution.py:602
Async XLA Ops:
  129.6 72.3 %copy-start = (bf16[768,2048]{1,0:T(8,128)(2,1)S(1)}, bf16[768,2048]{1,0:T(8,128)(2,1)}, u32[]{:S(2)}) copy-start(bf16[768,2048]{1,0:T(8,128)(2,1)} %w_ref.1) | copy-start | bytes 9437188

commit v3 on v2

--- a/solution.py
+++ b/solution.py
@@ -345,19 +345,25 @@
     )(ret_query, ret_key, ret_value, gate, turned, kv_weight)
 
 
-def gradient_kernel(
+def attention_kernel(
     n_sec,
     n_ctx,
-    kg_ref,
-    vg_ref,
+    q_ref,
+    g_ref,
+    k_ref,
+    v_ref,
+    att_ref,
+    qg_ref,
     out_ref,
+    send_sib,
+    keep,
     from_sib,
-    send_chip,
     got_chip,
     kept,
     send_part,
     got_part,
     final,
+    gathered,
     sib_send,
     sib_recv,
     chip_send,
@@ -371,156 +377,59 @@
     chip, core = lax.div(ctx, 2), lax.rem(ctx, 2)
     n_chip = n_ctx // 2
     sibling = (sec, chip * 2 + 1 - core)
-    rows = out_ref.shape[0]
-    pair = 2 * rows
-    half = kg_ref.shape[1]
-    piece = half // n_sec
-
-    others = [(lax.rem(sec + j, n_sec), chip * 2 + lax.rem(core + c, 2), j, c)
-              for j in range(n_sec) for c in range(2) if j or c]
-    greet(
-        [(s, d) for s, d, _, _ in others]
-        + [(sec, lax.rem(ctx + 2 * i, n_ctx)) for i in range(1, n_chip)]
-    )
-
-    def sib_copy(r, ref):
-        return remote(
-            ref.at[r * pair : (r + 1) * pair, :], from_sib.at[r], sib_send.at[r], sib_recv.at[r],
-            sibling,
-        )
-
-    for r in range(n_chip):
-
-        @pl.when(jnp.logical_and(r <= chip, core == 0))
-        def _():
-            sib_copy(r, vg_ref).start()
-
-        @pl.when(jnp.logical_and(r <= chip, core == 1))
-        def _():
-            sib_copy(r, kg_ref).start()
-
-    def chip_copy(r):
-        return remote(
-            send_chip.at[r], got_chip.at[chip], chip_send.at[r], chip_recv.at[chip],
-            (sec, 2 * r + core),
-        )
-
-    for r in range(n_chip):
-
-        @pl.when(r <= chip)
-        def _():
-            sib_copy(r, kg_ref).wait_recv()
-            cut = slice(r * pair, (r + 1) * pair)
-
-            @pl.when(core == 0)
-            def _():
-                kept[...] = kg_ref[cut, :].astype(jnp.float32) + from_sib[r].astype(jnp.float32)
-
-            @pl.when(core == 1)
-            def _():
-                kept[...] = vg_ref[cut, :].astype(jnp.float32) + from_sib[r].astype(jnp.float32)
-
-            @pl.when(r < chip)
-            def _():
-                send_chip[r] = kept[...].astype(jnp.bfloat16)
-                chip_copy(r).start()
-
-    for r in range(1, n_chip):
-
-        @pl.when(r > chip)
-        def _():
-            remote(
-                send_chip.at[r], got_chip.at[r], chip_send.at[r], chip_recv.at[r], sibling
-            ).wait_recv()
-            kept[...] += got_chip[r].astype(jnp.float32)
-
-    def part_copy(j):
-        return remote(
-            send_part.at[j - 1], got_part.at[j - 1], part_send.at[j - 1], part_recv.at[j - 1],
-            (lax.rem(sec + j, n_sec), ctx),
-        )
-
-    def cut_of(s):
-        return pl.ds(pl.multiple_of(s * piece, piece), piece)
-
-    for j in range(1, n_sec):
-        send_part[j - 1] = kept[:, cut_of(lax.rem(sec + j, n_sec))].astype(jnp.bfloat16)
-        part_copy(j).start()
-    summed = kept[:, cut_of(sec)]
-    for j in range(1, n_sec):
-        part_copy(j).wait_recv()
-        summed += got_part[j - 1].astype(jnp.float32)
-    final[...] = summed.astype(jnp.bfloat16)
-    place = pl.ds(pl.multiple_of(core * half + sec * piece, piece), piece)
-
-    def all_copy(s, d, j, c):
-        part = pl.ds(pl.multiple_of(lax.rem(core + c, 2) * rows, rows), rows)
-        return remote(
-            final.at[part, :], out_ref.at[:, place], all_send.at[j, c], all_recv.at[j, c], (s, d)
-        )
-
-    for s, d, j, c in others:
-        all_copy(s, d, j, c).start()
-    out_ref[:, place] = final[pl.ds(pl.multiple_of(core * rows, rows), rows), :]
-    for s, d, j, c in others:
-        all_copy(s, d, j, c).wait_recv()
-    for s, d, j, c in others:
-        all_copy(s, d, j, c).wait_send()
-    for j in range(1, n_sec):
-        part_copy(j).wait_send()
-    for r in range(n_chip):
-
-        @pl.when(r <= chip)
-        def _():
-            sib_copy(r, kg_ref).wait_send()
-
-        @pl.when(r < chip)
-        def _():
-            chip_copy(r).wait_send()
-
-
-def summed_gradient(key_grad, value_grad):
-    n_sec, n_ctx = lax.axis_size("section"), lax.axis_size("ctx")
-    n_chip = n_ctx // 2
-    total, half = key_grad.shape
-    rows = total // n_ctx
-    pair = 2 * rows
-    piece = half // n_sec
-    dma = pltpu.SemaphoreType.DMA
-    vmem = pl.BlockSpec(memory_space=pltpu.VMEM)
-    chips = pltpu.VMEM((n_chip, pair, half), jnp.bfloat16)
-    parts = pltpu.VMEM((n_sec - 1, pair, piece), jnp.bfloat16)
-    return pl.pallas_call(
-        functools.partial(gradient_kernel, n_sec, n_ctx),
-        out_shape=jax.ShapeDtypeStruct((rows, 2 * half), jnp.bfloat16),
-        in_specs=[vmem] * 2,
-        out_specs=vmem,
-        scratch_shapes=[
-            chips, chips, chips,
-            pltpu.VMEM((pair, half), jnp.float32),
-            parts, parts,
-            pltpu.VMEM((pair, piece), jnp.bfloat16),
-            dma((n_chip,)), dma((n_chip,)),
-            dma((n_chip,)), dma((n_chip,)),
-            dma((n_sec - 1,)), dma((n_sec - 1,)),
-            dma((n_sec, 2)), dma((n_sec, 2)),
-        ],
-        compiler_params=pltpu.CompilerParams(
-            collective_id=1, has_side_effects=True, vmem_limit_bytes=LIMIT
-        ),
-    )(key_grad, value_grad)
-
-
-def attention_kernel(ctx_ref, q_ref, g_ref, k_ref, v_ref, att_ref, qg_ref, kg_ref, vg_ref):
+    step = pl.program_id(0)
+    kv_heads = kept.shape[0]
+    part_heads = kv_heads // n_sec
     layer_count, row_count, width = q_ref.shape
     group = width // DH
     total = k_ref.shape[0]
-    columns = group * row_count
+    pair = 2 * row_count
     scale = 1.0 / math.sqrt(DH)
+
+    others = [
+        (lax.rem(sec + j, n_sec), chip * 2 + lax.rem(core + c, 2), j, c)
+        for j in range(n_sec)
+        for c in range(2)
+        if j or c
+    ]
+
+    @pl.when(step == 0)
+    def _():
+        greet(
+            [(s, d) for s, d, _, _ in others]
+            + [(sec, lax.rem(ctx + 2 * i, n_ctx)) for i in range(1, n_chip)]
+        )
+
+    def sib_copy(h):
+        return remote(send_sib.at[h], from_sib.at[h], sib_send.at[h], sib_recv.at[h], sibling)
+
+    def chip_copy(r, h):
+        return remote(
+            keep.at[h, r * pair : (r + 1) * pair, :],
+            got_chip.at[chip, h],
+            chip_send.at[r, h],
+            chip_recv.at[chip, h],
+            (sec, 2 * r + core),
+        )
+
+    def pass_on(h):
+        sib_copy(h).wait_recv()
+        mine = pl.ds(pl.multiple_of(chip * pair, pair), pair)
+        kept[h] = keep[h, mine, :].astype(jnp.float32) + from_sib[h, mine, :].astype(jnp.float32)
+        for r in range(n_chip - 1):
+
+            @pl.when(r < chip)
+            def _():
+                cut = slice(r * pair, (r + 1) * pair)
+                keep[h, cut, :] = (
+                    keep[h, cut, :].astype(jnp.float32) + from_sib[h, cut, :].astype(jnp.float32)
+                ).astype(jnp.bfloat16)
+                chip_copy(r, h).start()
+
     keys = k_ref[...]
     values = v_ref[...]
     key_place = lax.broadcasted_iota(jnp.int32, (total, row_count), 0)
-    row_place = ctx_ref[0] * row_count + lax.broadcasted_iota(jnp.int32, (total, row_count), 1)
+    row_place = ctx * row_count + lax.broadcasted_iota(jnp.int32, (total, row_count), 1)
     visible = jnp.concatenate([jnp.where(key_place <= row_place, 0.0, -jnp.inf)] * group, axis=1)
 
     def stacked(ref, layer):
@@ -561,44 +470,141 @@
         spread(qg_ref, layer, query_grad.astype(jnp.bfloat16))
         key_grad += jnp.dot(score_grad, queries, preferred_element_type=jnp.float32)
         value_grad += jnp.dot(low, grads, preferred_element_type=jnp.float32)
-    kg_ref[...] = key_grad.astype(kg_ref.dtype)
-    vg_ref[...] = value_grad.astype(vg_ref.dtype)
-
-
-def cross_attention(queries, cotangent, full_cache, place):
+        if layer == 0:
+
+            @pl.when(step > 0)
+            def _():
+                pass_on(step - 1)
+
+    key_low = key_grad.astype(jnp.bfloat16)
+    value_low = value_grad.astype(jnp.bfloat16)
+
+    @pl.when(core == 0)
+    def _():
+        keep[step] = key_low
+        send_sib[step] = value_low
+
+    @pl.when(core == 1)
+    def _():
+        keep[step] = value_low
+        send_sib[step] = key_low
+
+    sib_copy(step).start()
+
+    def part_copy(j):
+        return remote(
+            send_part.at[j - 1],
+            got_part.at[j - 1],
+            part_send.at[j - 1],
+            part_recv.at[j - 1],
+            (lax.rem(sec + j, n_sec), ctx),
+        )
+
+    piece = part_heads * DH
+    place = pl.ds(pl.multiple_of(core * kv_heads * DH + sec * piece, piece), piece)
+
+    def all_copy(s, d, j, c):
+        part = pl.ds(pl.multiple_of(lax.rem(core + c, 2) * row_count, row_count), row_count)
+        return remote(
+            final.at[part, :], gathered.at[:, place], all_send.at[j, c], all_recv.at[j, c], (s, d)
+        )
+
+    @pl.when(step == kv_heads - 1)
+    def _():
+        pass_on(kv_heads - 1)
+        for h in range(kv_heads):
+            for r in range(1, n_chip):
+
+                @pl.when(r > chip)
+                def _():
+                    remote(
+                        keep.at[h, 0:pair, :],
+                        got_chip.at[r, h],
+                        chip_send.at[r, h],
+                        chip_recv.at[r, h],
+                        sibling,
+                    ).wait_recv()
+                    kept[h] += got_chip[r, h].astype(jnp.float32)
+
+        for j in range(1, n_sec):
+            first = lax.rem(sec + j, n_sec) * part_heads
+            for i in range(part_heads):
+                send_part[j - 1, :, i * DH : (i + 1) * DH] = kept[first + i].astype(jnp.bfloat16)
+            part_copy(j).start()
+        for j in range(1, n_sec):
+            part_copy(j).wait_recv()
+        for i in range(part_heads):
+            cut = slice(i * DH, (i + 1) * DH)
+            summed = kept[sec * part_heads + i]
+            for j in range(1, n_sec):
+                summed += got_part[j - 1, :, cut].astype(jnp.float32)
+            final[:, cut] = summed.astype(jnp.bfloat16)
+        for s, d, j, c in others:
+            all_copy(s, d, j, c).start()
+        own = pl.ds(pl.multiple_of(core * row_count, row_count), row_count)
+        gathered[:, place] = final[own, :]
+        for s, d, j, c in others:
+            all_copy(s, d, j, c).wait_recv()
+        out_ref[...] = gathered[...]
+        for s, d, j, c in others:
+            all_copy(s, d, j, c).wait_send()
+        for j in range(1, n_sec):
+            part_copy(j).wait_send()
+        for h in range(kv_heads):
+            sib_copy(h).wait_send()
+            for r in range(n_chip - 1):
+
+                @pl.when(r < chip)
+                def _():
+                    chip_copy(r, h).wait_send()
+
+
+def cross_attention(queries, cotangent, full_cache):
+    n_sec, n_ctx = lax.axis_size("section"), lax.axis_size("ctx")
+    n_chip = n_ctx // 2
     layer_count, row_count, model_width = queries.shape
     total, cache_width = full_cache.shape
     kv_heads = cache_width // 2 // DH
     width = model_width // kv_heads
-    rows = pl.BlockSpec((layer_count, row_count, width), lambda h, c: (0, 0, h))
-    cut = pl.BlockSpec((total, DH), lambda h, c: (0, h))
-    cut_values = pl.BlockSpec((total, DH), lambda h, c: (0, kv_heads + h))
-    half = jax.ShapeDtypeStruct((total, cache_width // 2), jnp.bfloat16)
+    pair = 2 * row_count
+    piece = kv_heads // n_sec * DH
+    rows = pl.BlockSpec((layer_count, row_count, width), lambda h: (0, 0, h))
+    cut = pl.BlockSpec((total, DH), lambda h: (0, h))
+    cut_values = pl.BlockSpec((total, DH), lambda h: (0, kv_heads + h))
+    dma = pltpu.SemaphoreType.DMA
+    per_head = pltpu.VMEM((kv_heads, total, DH), jnp.bfloat16)
+    parts = pltpu.VMEM((n_sec - 1, pair, piece), jnp.bfloat16)
     return pl.pallas_call(
-        attention_kernel,
-        grid_spec=pltpu.PrefetchScalarGridSpec(
-            num_scalar_prefetch=1,
-            grid=(kv_heads,),
-            in_specs=[rows, rows, cut, cut_values],
-            out_specs=[rows, rows, cut, cut],
-        ),
+        functools.partial(attention_kernel, n_sec, n_ctx),
+        grid=(kv_heads,),
+        in_specs=[rows, rows, cut, cut_values],
+        out_specs=[rows, rows, pl.BlockSpec((row_count, cache_width), lambda h: (0, 0))],
         out_shape=[
             jax.ShapeDtypeStruct(queries.shape, jnp.bfloat16),
             jax.ShapeDtypeStruct(queries.shape, jnp.bfloat16),
-            half,
-            half,
+            jax.ShapeDtypeStruct((row_count, cache_width), jnp.bfloat16),
         ],
-        compiler_params=pltpu.CompilerParams(vmem_limit_bytes=LIMIT),
-    )(place, queries, cotangent, full_cache, full_cache)
+        scratch_shapes=[
+            per_head, per_head, per_head,
+            pltpu.VMEM((n_chip, kv_heads, pair, DH), jnp.bfloat16),
+            pltpu.VMEM((kv_heads, pair, DH), jnp.float32),
+            parts, parts,
+            pltpu.VMEM((pair, piece), jnp.bfloat16),
+            pltpu.VMEM((row_count, cache_width), jnp.bfloat16),
+            dma((kv_heads,)), dma((kv_heads,)),
+            dma((n_chip, kv_heads)), dma((n_chip, kv_heads)),
+            dma((n_sec - 1,)), dma((n_sec - 1,)),
+            dma((n_sec, 2)), dma((n_sec, 2)),
+        ],
+        compiler_params=pltpu.CompilerParams(
+            collective_id=1, has_side_effects=True, vmem_limit_bytes=LIMIT
+        ),
+    )(queries, cotangent, full_cache, full_cache)
 
 
 def body(queries, cotangent, ret_query, ret_key, ret_value, gate_log, kv_weight):
     full_cache = shared_cache(ret_query, ret_key, ret_value, gate_log, kv_weight)
-    place = lax.axis_index("ctx").reshape(1)
-    attended_all, grad_rows_all, key_grad, value_grad = cross_attention(
-        queries, cotangent, full_cache, place
-    )
-    cache_grad = summed_gradient(key_grad, value_grad)
+    attended_all, grad_rows_all, cache_grad = cross_attention(queries, cotangent, full_cache)
     retention_grad = jnp.einsum(
         "rw,cw->rc", cache_grad, kv_weight, preferred_element_type=jnp.float32
     ).astype(jnp.bfloat16)

time: 208 us -> 193 us (0.928)
  Pallas kernels: 198 us -> 179 us
  local copies, waits for them, and re-layouts: 2.75 us -> 6.28 us
    pallas_call x2 -> x1, Pallas kernels: 129 us -> 110 us  [cross_attention(): pl.pallas_call(functools.partial(attention_kernel, n_sec, n_ctx), grid=(k...]
    unnamed x3 -> x9, local copies, waits for them, and re-layouts: 0.8 us -> 4.33 us
where the time goes in v3:
time: 193 us; the launch traced here: 189 us
  Pallas kernels  179 us (93%)
  local copies, waits for them, and re-layouts  6.28 us (3%)
  matrix products  3.11 us (2%)
    pallas_call x1, Pallas kernels, cross_attention(): pl.pallas_call(functools.partial(attention_kernel, n_sec, n_ctx), grid=(k...  110 us
    pallas_call x1, Pallas kernels, shared_cache(): pl.pallas_call(functools.partial(cache_kernel, n_sec, n_ctx), out_shape=j...  69.2 us
    unnamed x9, local copies, waits for them, and re-layouts  4.33 us

profile of v3, /device:TPU:0, one launch (start us, length us, event | category | flops | bytes accessed | tf_op | source)
XLA Modules:
  0.0 189.1 jit_solution(1275349713060137213)
XLA Ops:
  0.6 1.3 pad.9.turned_ref
  1.9 0.8 copy.10
  2.7 0.6 pad.8.gate_ref
  3.4 69.2 %shard_map.94.k_ref.v_ref = bf16[1280,2048]{1,0:T(8,128)(2,1)} custom-call(bf16[160,768]{1,0:T(8,128)(2,1)} %q_ref.2, bf16[160,768]{1,0:T(8,128)(2,1)} %k_ref.1, bf16[160,768]{1,0:T(8,128)(2,1)} %v_ref.1, f32[160,128]{1,0:T(8,128)} %pad.8.gate_ref, f32[8,160]{1,0:T(8,128)} %pad.9.turned_ref, bf16[768,2048]{1,0:T(8,128)(2,1)} %w_ref.1), custom_call_target="tpu_custom_call" | custom-call | tf_op jit(solution)/shard_map/pallas_call | solution.py:320
  72.6 0.0 copy-start
  72.6 109.8 %shard_map.95 = (bf16[2,160,3072]{2,1,0:T(8,128)(2,1)}, bf16[2,160,3072]{2,1,0:T(8,128)(2,1)}, bf16[160,2048]{1,0:T(8,128)(2,1)}) custom-call(bf16[2,160,3072]{2,1,0:T(8,128)(2,1)} %q_ref.3, bf16[2,160,3072]{2,1,0:T(8,128)(2,1)} %g_ref.1, bf16[1280,2048]{1,0:T(8,128)(2,1)} %shard_map.94.k_ref.v_ref, bf16[1280,2048]{1,0:T(8,128)(2,1)} %shard_map.94.k_ref.v_ref), custom_call_target="tpu_custom_call" | custom-call | tf_op jit(solution)/shard_map/pallas_call | solution.py:577
  182.5 0.0 copy-done
  182.5 0.0 copy-start.2
  182.5 3.1 %convolution_convert_fusion = bf16[160,768]{1,0:T(8,128)(2,1)} fusion(bf16[160,2048]{1,0:T(8,128)(2,1)} %get-tuple-element.8, bf16[768,2048]{1,0:T(8,128)(2,1)S(1)} %copy-done), kind=kOutput, calls=%fused_computation | convolution fusion | flops 503439360 | bytes 4046848 | tf_op jit(solution)/shard_map/rw,cw->rc/dot_general | solution.py:608
  185.6 0.0 copy-done.2
  185.6 0.0 copy-start.1
  185.6 1.3 copy.13
  186.9 1.0 copy-done.1
  187.8 1.3 copy.14
Async XLA Ops:
  72.6 109.9 %copy-start = (bf16[768,2048]{1,0:T(8,128)(2,1)S(1)}, bf16[768,2048]{1,0:T(8,128)(2,1)}, u32[]{:S(2)}) copy-start(bf16[768,2048]{1,0:T(8,128)(2,1)} %w_ref.1) | copy-start | bytes 9437188
  182.5 3.1 %copy-start.2 = (bf16[2,160,3072]{2,1,0:T(8,128)(2,1)S(1)}, bf16[2,160,3072]{2,1,0:T(8,128)(2,1)}, u32[]{:S(2)}) copy-start(bf16[2,160,3072]{2,1,0:T(8,128)(2,1)} %get-tuple-element.12) | copy-start | bytes 5898244
  185.6 2.3 %copy-start.1 = (bf16[2,160,3072]{2,1,0:T(8,128)(2,1)S(1)}, bf16[2,160,3072]{2,1,0:T(8,128)(2,1)}, u32[]{:S(2)}) copy-start(bf16[2,160,3072]{2,1,0:T(8,128)(2,1)} %get-tuple-element.13) | copy-start | bytes 5898244

commit v4 on v3

--- a/solution.py
+++ b/solution.py
@@ -90,7 +90,6 @@
     heads = width // DH
     columns = out_ref.shape[1]
     piece = columns // n_sec
-    half = columns // 2
     row_dims = (((0,), (0,)), ((), ()))
     plain = (((1,), (0,)), ((), ()))
     last_dims = (((1,), (1,)), ((), ()))
@@ -230,68 +229,85 @@
         spot = out_ref.at[my_rows, my_cut]
         return remote(spot, spot, z_send.at[j - 1], z_recv.at[j - 1], (lax.rem(sec + j, n_sec), ctx))
 
+    def section_at(j):
+        return lax.rem(sec + n_sec - j, n_sec)
+
+    def cut_of(s):
+        return pl.ds(pl.multiple_of(s * piece, piece), piece)
+
+    def core_of(s):
+        return lax.div(s * 2, n_sec)
+
+    def x_copy(r, s):
+        spot = out_ref.at[my_rows, cut_of(s)]
+        return remote(
+            spot, spot, x_send.at[r, s], x_recv.at[ctx, s], (sec, 2 * r + core_of(s))
+        )
+
+    def y_copy(d, s):
+        spot = out_ref.at[d * rows : (d + 1) * rows, cut_of(s)]
+        return remote(spot, spot, y_send.at[d, s], y_recv.at[d, s], sibling)
+
+    def own_copy(s):
+        spot = out_ref.at[my_rows, cut_of(s)]
+        return remote(spot, spot, y_send.at[n_ctx, s], y_recv.at[n_ctx, s], sibling)
+
     for j in range(1, n_sec):
         z_copy(j).start()
-    for j in range(1, n_sec):
-        z_copy(j).wait_recv()
-
-    def x_copy(r, c):
-        spot = out_ref.at[my_rows, c * half : (c + 1) * half]
-        return remote(spot, spot, x_send.at[r, c], x_recv.at[ctx], (sec, 2 * r + c))
-
-    def y_copy(d, c, cut, device):
-        spot = out_ref.at[d * rows : (d + 1) * rows, cut]
-        return remote(spot, spot, y_send.at[d], y_recv.at[d], device)
-
-    for r in range(n_chip - 1, 0, -1):
+    for j in range(n_sec):
+        s = section_at(j)
+        if j:
+            z_copy(j).wait_recv()
+        for r in range(n_chip - 1, 0, -1):
+
+            @pl.when(r > chip)
+            def _():
+                x_copy(r, s).start()
+
+        @pl.when(core == 0)
+        def _():
+            own_copy(s).start()
+
+    for j in range(n_sec):
+        s = section_at(j)
+        for d in range(n_ctx - 3, -1, -1):
+
+            @pl.when(jnp.logical_and(d < chip * 2, core_of(s) == core))
+            def _():
+                spot = out_ref.at[d * rows : (d + 1) * rows, cut_of(s)]
+                remote(spot, spot, x_send.at[0, 0], x_recv.at[d, s], sibling).wait_recv()
+                y_copy(d, s).start()
+
+    for s in range(n_sec):
+        for d in range(n_ctx - 2):
+
+            @pl.when(jnp.logical_and(d < chip * 2, core_of(s) != core))
+            def _():
+                y_copy(d, s).wait_recv()
+
+            @pl.when(jnp.logical_and(d < chip * 2, core_of(s) == core))
+            def _():
+                y_copy(d, s).wait_send()
+
+    @pl.when(core == 0)
+    def _():
+        for s in range(n_sec):
+            own_copy(s).wait_send()
+        to_sibling(0).wait_send()
+        to_sibling(1).wait_send()
+
+    @pl.when(core == 1)
+    def _():
+        for s in range(n_sec):
+            spot = out_ref.at[pl.ds(pl.multiple_of((ctx - core) * rows, rows), rows), cut_of(s)]
+            remote(spot, spot, y_send.at[n_ctx, s], y_recv.at[n_ctx, s], sibling).wait_recv()
+
+    for r in range(1, n_chip):
 
         @pl.when(r > chip)
         def _():
-            for c in range(2):
-                x_copy(r, c).start()
-
-    def own_copy():
-        spot = out_ref.at[my_rows, :]
-        return remote(spot, spot, y_send.at[n_ctx], y_recv.at[n_ctx], sibling)
-
-    @pl.when(core == 0)
-    def _():
-        own_copy().start()
-
-    my_half = pl.ds(pl.multiple_of(core * half, half), half)
-    for d in range(n_ctx - 3, -1, -1):
-
-        @pl.when(d < chip * 2)
-        def _():
-            spot = out_ref.at[d * rows : (d + 1) * rows, my_half]
-            remote(spot, spot, x_send.at[0, 0], x_recv.at[d], sibling).wait_recv()
-            y_copy(d, core, my_half, sibling).start()
-
-    other_half = pl.ds(pl.multiple_of((1 - core) * half, half), half)
-    for d in range(n_ctx - 2):
-
-        @pl.when(d < chip * 2)
-        def _():
-            y_copy(d, core, other_half, sibling).wait_recv()
-            y_copy(d, core, my_half, sibling).wait_send()
-
-    @pl.when(core == 0)
-    def _():
-        own_copy().wait_send()
-        to_sibling(0).wait_send()
-        to_sibling(1).wait_send()
-
-    @pl.when(core == 1)
-    def _():
-        spot = out_ref.at[pl.ds(pl.multiple_of((ctx - core) * rows, rows), rows), :]
-        remote(spot, spot, y_send.at[n_ctx], y_recv.at[n_ctx], sibling).wait_recv()
-
-    for r in range(1, n_chip):
-
-        @pl.when(r > chip)
-        def _():
-            for c in range(2):
-                x_copy(r, c).wait_send()
+            for s in range(n_sec):
+                x_copy(r, s).wait_send()
 
             @pl.when(core == 1)
             def _():
@@ -336,8 +352,8 @@
             dma((n_chip, 2)), dma((n_chip,)),
             dma((n_sec - 1,)), dma((n_sec - 1,)),
             dma((n_sec - 1,)), dma((n_sec - 1,)),
-            dma((n_chip, 2)), dma((n_ctx,)),
-            dma((n_ctx + 1,)), dma((n_ctx + 1,)),
+            dma((n_chip, n_sec)), dma((n_ctx, n_sec)),
+            dma((n_ctx + 1, n_sec)), dma((n_ctx + 1, n_sec)),
         ],
         compiler_params=pltpu.CompilerParams(
             collective_id=0, has_side_effects=True, vmem_limit_bytes=LIMIT
@@ -426,8 +442,74 @@
                 ).astype(jnp.bfloat16)
                 chip_copy(r, h).start()
 
+    def place_of(h, c):
+        return pl.ds(pl.multiple_of((c * kv_heads + h) * DH, DH), DH)
+
+    def part_copy(h):
+        owner = lax.div(h, part_heads)
+        return remote(
+            send_part.at[h],
+            got_part.at[sec, h - owner * part_heads],
+            part_send.at[h],
+            part_recv.at[sec, h - owner * part_heads],
+            (owner, ctx),
+        )
+
+    def collect(h):
+        for r in range(1, n_chip):
+
+            @pl.when(r > chip)
+            def _():
+                remote(
+                    keep.at[h, 0:pair, :],
+                    got_chip.at[r, h],
+                    chip_send.at[r, h],
+                    chip_recv.at[r, h],
+                    sibling,
+                ).wait_recv()
+                kept[h] += got_chip[r, h].astype(jnp.float32)
+
+        @pl.when(sec != lax.div(h, part_heads))
+        def _():
+            send_part[h] = kept[h].astype(jnp.bfloat16)
+            part_copy(h).start()
+
+    def all_copy(h, s, d, j, c):
+        index = h - sec * part_heads
+        part = pl.ds(pl.multiple_of(lax.rem(core + c, 2) * row_count, row_count), row_count)
+        return remote(
+            final.at[index, part, :],
+            gathered.at[:, place_of(h, core)],
+            all_send.at[index, j, c],
+            all_recv.at[h, core],
+            (s, d),
+        )
+
+    def finish(h):
+        @pl.when(sec == lax.div(h, part_heads))
+        def _():
+            index = h - sec * part_heads
+            summed = kept[h]
+            for j in range(1, n_sec):
+                s = lax.rem(sec + j, n_sec)
+                remote(
+                    send_part.at[h],
+                    got_part.at[s, index],
+                    part_send.at[h],
+                    part_recv.at[s, index],
+                    sibling,
+                ).wait_recv()
+                summed += got_part[s, index].astype(jnp.float32)
+            final[index] = summed.astype(jnp.bfloat16)
+            for s, d, j, c in others:
+                all_copy(h, s, d, j, c).start()
+            own = pl.ds(pl.multiple_of(core * row_count, row_count), row_count)
+            gathered[:, place_of(h, core)] = final[index, own, :]
+
     keys = k_ref[...]
     values = v_ref[...]
+    keys_turned = keys.T
+    values_turned = values.T
     key_place = lax.broadcasted_iota(jnp.int32, (total, row_count), 0)
     row_place = ctx * row_count + lax.broadcasted_iota(jnp.int32, (total, row_count), 1)
     visible = jnp.concatenate([jnp.where(key_place <= row_place, 0.0, -jnp.inf)] * group, axis=1)
@@ -454,9 +536,8 @@
         soft = jnp.exp(scores - top)
         soft = soft * (1.0 / jnp.sum(soft, axis=0, keepdims=True))
         low = soft.astype(jnp.bfloat16)
-        mixed = lax.dot_general(
-            low, values, (((0,), (0,)), ((), ())), preferred_element_type=jnp.float32
-        ).astype(jnp.bfloat16)
+        mixed = jnp.dot(values_turned, low, preferred_element_type=jnp.float32)
+        mixed = mixed.T.astype(jnp.bfloat16)
         spread(att_ref, layer, mixed)
         product = grads.astype(jnp.float32) * mixed.astype(jnp.float32)
         delta = jnp.sum(product.T, axis=0, keepdims=True)
@@ -464,10 +545,8 @@
             values, grads, (((1,), (1,)), ((), ())), preferred_element_type=jnp.float32
         )
         score_grad = (soft * (prob_grad - delta) * scale).astype(jnp.bfloat16)
-        query_grad = lax.dot_general(
-            score_grad, keys, (((0,), (0,)), ((), ())), preferred_element_type=jnp.float32
-        )
-        spread(qg_ref, layer, query_grad.astype(jnp.bfloat16))
+        query_grad = jnp.dot(keys_turned, score_grad, preferred_element_type=jnp.float32)
+        spread(qg_ref, layer, query_grad.T.astype(jnp.bfloat16))
         key_grad += jnp.dot(score_grad, queries, preferred_element_type=jnp.float32)
         value_grad += jnp.dot(low, grads, preferred_element_type=jnp.float32)
         if layer == 0:
@@ -476,6 +555,14 @@
             def _():
                 pass_on(step - 1)
 
+            @pl.when(step > 1)
+            def _():
+                collect(step - 2)
+
+            @pl.when(step > 2)
+            def _():
+                finish(step - 3)
+
     key_low = key_grad.astype(jnp.bfloat16)
     value_low = value_grad.astype(jnp.bfloat16)
 
@@ -491,65 +578,27 @@
 
     sib_copy(step).start()
 
-    def part_copy(j):
-        return remote(
-            send_part.at[j - 1],
-            got_part.at[j - 1],
-            part_send.at[j - 1],
-            part_recv.at[j - 1],
-            (lax.rem(sec + j, n_sec), ctx),
-        )
-
-    piece = part_heads * DH
-    place = pl.ds(pl.multiple_of(core * kv_heads * DH + sec * piece, piece), piece)
-
-    def all_copy(s, d, j, c):
-        part = pl.ds(pl.multiple_of(lax.rem(core + c, 2) * row_count, row_count), row_count)
-        return remote(
-            final.at[part, :], gathered.at[:, place], all_send.at[j, c], all_recv.at[j, c], (s, d)
-        )
-
     @pl.when(step == kv_heads - 1)
     def _():
         pass_on(kv_heads - 1)
+        for h in range(max(kv_heads - 2, 0), kv_heads):
+            collect(h)
+        for h in range(max(kv_heads - 3, 0), kv_heads):
+            finish(h)
         for h in range(kv_heads):
-            for r in range(1, n_chip):
-
-                @pl.when(r > chip)
+            for c in range(2):
+
+                @pl.when(jnp.logical_or(sec != h // part_heads, core != c))
                 def _():
                     remote(
-                        keep.at[h, 0:pair, :],
-                        got_chip.at[r, h],
-                        chip_send.at[r, h],
-                        chip_recv.at[r, h],
+                        final.at[0, 0:row_count, :],
+                        gathered.at[:, place_of(h, c)],
+                        all_send.at[0, 0, 0],
+                        all_recv.at[h, c],
                         sibling,
                     ).wait_recv()
-                    kept[h] += got_chip[r, h].astype(jnp.float32)
-
-        for j in range(1, n_sec):
-            first = lax.rem(sec + j, n_sec) * part_heads
-            for i in range(part_heads):
-                send_part[j - 1, :, i * DH : (i + 1) * DH] = kept[first + i].astype(jnp.bfloat16)
-            part_copy(j).start()
-        for j in range(1, n_sec):
-            part_copy(j).wait_recv()
-        for i in range(part_heads):
-            cut = slice(i * DH, (i + 1) * DH)
-            summed = kept[sec * part_heads + i]
-            for j in range(1, n_sec):
-                summed += got_part[j - 1, :, cut].astype(jnp.float32)
-            final[:, cut] = summed.astype(jnp.bfloat16)
-        for s, d, j, c in others:
-            all_copy(s, d, j, c).start()
-        own = pl.ds(pl.multiple_of(core * row_count, row_count), row_count)
-        gathered[:, place] = final[own, :]
-        for s, d, j, c in others:
-            all_copy(s, d, j, c).wait_recv()
+
         out_ref[...] = gathered[...]
-        for s, d, j, c in others:
-            all_copy(s, d, j, c).wait_send()
-        for j in range(1, n_sec):
-            part_copy(j).wait_send()
         for h in range(kv_heads):
             sib_copy(h).wait_send()
             for r in range(n_chip - 1):
@@ -557,6 +606,15 @@
                 @pl.when(r < chip)
                 def _():
                     chip_copy(r, h).wait_send()
+
+            @pl.when(sec != h // part_heads)
+            def _():
+                part_copy(h).wait_send()
+
+            @pl.when(sec == h // part_heads)
+            def _():
+                for s, d, j, c in others:
+                    all_copy(h, s, d, j, c).wait_send()
 
 
 def cross_attention(queries, cotangent, full_cache):
@@ -567,13 +625,12 @@
     kv_heads = cache_width // 2 // DH
     width = model_width // kv_heads
     pair = 2 * row_count
-    piece = kv_heads // n_sec * DH
+    part_heads = kv_heads // n_sec
     rows = pl.BlockSpec((layer_count, row_count, width), lambda h: (0, 0, h))
     cut = pl.BlockSpec((total, DH), lambda h: (0, h))
     cut_values = pl.BlockSpec((total, DH), lambda h: (0, kv_heads + h))
     dma = pltpu.SemaphoreType.DMA
     per_head = pltpu.VMEM((kv_heads, total, DH), jnp.bfloat16)
-    parts = pltpu.VMEM((n_sec - 1, pair, piece), jnp.bfloat16)
     return pl.pallas_call(
         functools.partial(attention_kernel, n_sec, n_ctx),
         grid=(kv_heads,),
@@ -588,13 +645,14 @@
             per_head, per_head, per_head,
             pltpu.VMEM((n_chip, kv_heads, pair, DH), jnp.bfloat16),
             pltpu.VMEM((kv_heads, pair, DH), jnp.float32),
-            parts, parts,
-            pltpu.VMEM((pair, piece), jnp.bfloat16),
+            pltpu.VMEM((kv_heads, pair, DH), jnp.bfloat16),
+            pltpu.VMEM((n_sec, part_heads, pair, DH), jnp.bfloat16),
+            pltpu.VMEM((part_heads, pair, DH), jnp.bfloat16),
             pltpu.VMEM((row_count, cache_width), jnp.bfloat16),
             dma((kv_heads,)), dma((kv_heads,)),
             dma((n_chip, kv_heads)), dma((n_chip, kv_heads)),
-            dma((n_sec - 1,)), dma((n_sec - 1,)),
-            dma((n_sec, 2)), dma((n_sec, 2)),
+            dma((kv_heads,)), dma((n_sec, part_heads)),
+            dma((part_heads, n_sec, 2)), dma((kv_heads, 2)),
         ],
         compiler_params=pltpu.CompilerParams(
             collective_id=1, has_side_effects=True, vmem_limit_bytes=LIMIT

time: 193 us -> 159 us (0.82)
  Pallas kernels: 179 us -> 146 us
    pallas_call x1, Pallas kernels: 110 us -> 83.7 us  [cross_attention(): pl.pallas_call(functools.partial(attention_kernel, n_sec, n_ctx), grid=(k...]
    pallas_call x1, Pallas kernels: 69.2 us -> 62.1 us  [shared_cache(): pl.pallas_call(functools.partial(cache_kernel, n_sec, n_ctx), out_shape=j...]
where the time goes in v4:
time: 159 us; the launch traced here: 156 us
  Pallas kernels  146 us (92%)
  local copies, waits for them, and re-layouts  6.28 us (4%)
  matrix products  3.11 us (2%)
    pallas_call x1, Pallas kernels, cross_attention(): pl.pallas_call(functools.partial(attention_kernel, n_sec, n_ctx), grid=(k...  83.7 us
    pallas_call x1, Pallas kernels, shared_cache(): pl.pallas_call(functools.partial(cache_kernel, n_sec, n_ctx), out_shape=j...  62.1 us
    unnamed x9, local copies, waits for them, and re-layouts  4.33 us

profile of v4, /device:TPU:0, one launch (start us, length us, event | category | flops | bytes accessed | tf_op | source)
XLA Modules:
  0.0 155.9 jit_solution(5250789123023380661)
XLA Ops:
  0.6 1.3 pad.9.turned_ref
  1.9 0.8 copy.10
  2.7 0.6 pad.8.gate_ref
  3.4 62.1 %shard_map.94.k_ref.v_ref = bf16[1280,2048]{1,0:T(8,128)(2,1)} custom-call(bf16[160,768]{1,0:T(8,128)(2,1)} %q_ref.2, bf16[160,768]{1,0:T(8,128)(2,1)} %k_ref.1, bf16[160,768]{1,0:T(8,128)(2,1)} %v_ref.1, f32[160,128]{1,0:T(8,128)} %pad.8.gate_ref, f32[8,160]{1,0:T(8,128)} %pad.9.turned_ref, bf16[768,2048]{1,0:T(8,128)(2,1)} %w_ref.1), custom_call_target="tpu_custom_call" | custom-call | tf_op jit(solution)/shard_map/pallas_call | solution.py:336
  65.5 0.0 copy-start
  65.5 83.7 %shard_map.95 = (bf16[2,160,3072]{2,1,0:T(8,128)(2,1)}, bf16[2,160,3072]{2,1,0:T(8,128)(2,1)}, bf16[160,2048]{1,0:T(8,128)(2,1)}) custom-call(bf16[2,160,3072]{2,1,0:T(8,128)(2,1)} %q_ref.3, bf16[2,160,3072]{2,1,0:T(8,128)(2,1)} %g_ref.1, bf16[1280,2048]{1,0:T(8,128)(2,1)} %shard_map.94.k_ref.v_ref, bf16[1280,2048]{1,0:T(8,128)(2,1)} %shard_map.94.k_ref.v_ref), custom_call_target="tpu_custom_call" | custom-call | tf_op jit(solution)/shard_map/pallas_call | solution.py:634
  149.2 0.0 copy-done
  149.3 0.0 copy-start.2
  149.3 3.1 %convolution_convert_fusion = bf16[160,768]{1,0:T(8,128)(2,1)} fusion(bf16[160,2048]{1,0:T(8,128)(2,1)} %get-tuple-element.8, bf16[768,2048]{1,0:T(8,128)(2,1)S(1)} %copy-done), kind=kOutput, calls=%fused_computation | convolution fusion | flops 503439360 | bytes 4046848 | tf_op jit(solution)/shard_map/rw,cw->rc/dot_general | solution.py:666
  152.4 0.0 copy-done.2
  152.4 0.0 copy-start.1
  152.4 1.3 copy.13
  153.7 1.0 copy-done.1
  154.6 1.3 copy.14
Async XLA Ops:
  65.5 83.7 %copy-start = (bf16[768,2048]{1,0:T(8,128)(2,1)S(1)}, bf16[768,2048]{1,0:T(8,128)(2,1)}, u32[]{:S(2)}) copy-start(bf16[768,2048]{1,0:T(8,128)(2,1)} %w_ref.1) | copy-start | bytes 9437188
  149.3 3.1 %copy-start.2 = (bf16[2,160,3072]{2,1,0:T(8,128)(2,1)S(1)}, bf16[2,160,3072]{2,1,0:T(8,128)(2,1)}, u32[]{:S(2)}) copy-start(bf16[2,160,3072]{2,1,0:T(8,128)(2,1)} %get-tuple-element.12) | copy-start | bytes 5898244
  152.4 2.3 %copy-start.1 = (bf16[2,160,3072]{2,1,0:T(8,128)(2,1)S(1)}, bf16[2,160,3072]{2,1,0:T(8,128)(2,1)}, u32[]{:S(2)}) copy-start(bf16[2,160,3072]{2,1,0:T(8,128)(2,1)} %get-tuple-element.13) | copy-start | bytes 5898244

commit v5 on v4

--- a/solution.py
+++ b/solution.py
@@ -77,10 +77,6 @@
     part_recv,
     z_send,
     z_recv,
-    x_send,
-    x_recv,
-    y_send,
-    y_recv,
 ):
     sec, ctx = lax.axis_index("section"), lax.axis_index("ctx")
     chip, core = lax.div(ctx, 2), lax.rem(ctx, 2)
@@ -212,103 +208,30 @@
         send_part[j - 1] = part_of(lax.rem(sec + j, n_sec)).astype(jnp.bfloat16)
         part_copy(j).start()
     summed = part_of(sec)
-    for r in range(1, n_ctx):
-
-        @pl.when(r > ctx)
-        def _():
-            out_ref[r * rows : (r + 1) * rows, :] = jnp.zeros((rows, columns), jnp.bfloat16)
-
     for j in range(1, n_sec):
         part_copy(j).wait_recv()
         summed += got_part[j - 1].astype(jnp.float32)
-    my_rows = pl.ds(pl.multiple_of(ctx * rows, rows), rows)
     my_cut = pl.ds(pl.multiple_of(sec * piece, piece), piece)
-    out_ref[my_rows, my_cut] = summed.astype(jnp.bfloat16)
+    out_ref[:, my_cut] = summed.astype(jnp.bfloat16)
 
     def z_copy(j):
-        spot = out_ref.at[my_rows, my_cut]
+        spot = out_ref.at[:, my_cut]
         return remote(spot, spot, z_send.at[j - 1], z_recv.at[j - 1], (lax.rem(sec + j, n_sec), ctx))
-
-    def section_at(j):
-        return lax.rem(sec + n_sec - j, n_sec)
-
-    def cut_of(s):
-        return pl.ds(pl.multiple_of(s * piece, piece), piece)
-
-    def core_of(s):
-        return lax.div(s * 2, n_sec)
-
-    def x_copy(r, s):
-        spot = out_ref.at[my_rows, cut_of(s)]
-        return remote(
-            spot, spot, x_send.at[r, s], x_recv.at[ctx, s], (sec, 2 * r + core_of(s))
-        )
-
-    def y_copy(d, s):
-        spot = out_ref.at[d * rows : (d + 1) * rows, cut_of(s)]
-        return remote(spot, spot, y_send.at[d, s], y_recv.at[d, s], sibling)
-
-    def own_copy(s):
-        spot = out_ref.at[my_rows, cut_of(s)]
-        return remote(spot, spot, y_send.at[n_ctx, s], y_recv.at[n_ctx, s], sibling)
 
     for j in range(1, n_sec):
         z_copy(j).start()
-    for j in range(n_sec):
-        s = section_at(j)
-        if j:
-            z_copy(j).wait_recv()
-        for r in range(n_chip - 1, 0, -1):
-
-            @pl.when(r > chip)
-            def _():
-                x_copy(r, s).start()
-
-        @pl.when(core == 0)
-        def _():
-            own_copy(s).start()
-
-    for j in range(n_sec):
-        s = section_at(j)
-        for d in range(n_ctx - 3, -1, -1):
-
-            @pl.when(jnp.logical_and(d < chip * 2, core_of(s) == core))
-            def _():
-                spot = out_ref.at[d * rows : (d + 1) * rows, cut_of(s)]
-                remote(spot, spot, x_send.at[0, 0], x_recv.at[d, s], sibling).wait_recv()
-                y_copy(d, s).start()
-
-    for s in range(n_sec):
-        for d in range(n_ctx - 2):
-
-            @pl.when(jnp.logical_and(d < chip * 2, core_of(s) != core))
-            def _():
-                y_copy(d, s).wait_recv()
-
-            @pl.when(jnp.logical_and(d < chip * 2, core_of(s) == core))
-            def _():
-                y_copy(d, s).wait_send()
+    for j in range(1, n_sec):
+        z_copy(j).wait_recv()
 
     @pl.when(core == 0)
     def _():
-        for s in range(n_sec):
-            own_copy(s).wait_send()
         to_sibling(0).wait_send()
         to_sibling(1).wait_send()
 
-    @pl.when(core == 1)
-    def _():
-        for s in range(n_sec):
-            spot = out_ref.at[pl.ds(pl.multiple_of((ctx - core) * rows, rows), rows), cut_of(s)]
-            remote(spot, spot, y_send.at[n_ctx, s], y_recv.at[n_ctx, s], sibling).wait_recv()
-
     for r in range(1, n_chip):
 
         @pl.when(r > chip)
         def _():
-            for s in range(n_sec):
-                x_copy(r, s).wait_send()
-
             @pl.when(core == 1)
             def _():
                 for c in range(2):
@@ -335,7 +258,7 @@
     vmem = pl.BlockSpec(memory_space=pltpu.VMEM)
     return pl.pallas_call(
         functools.partial(cache_kernel, n_sec, n_ctx),
-        out_shape=jax.ShapeDtypeStruct((n_ctx * rows, columns), jnp.bfloat16),
+        out_shape=jax.ShapeDtypeStruct((rows, columns), jnp.bfloat16),
         in_specs=[vmem] * 6,
         out_specs=vmem,
         scratch_shapes=[
@@ -352,8 +275,6 @@
             dma((n_chip, 2)), dma((n_chip,)),
             dma((n_sec - 1,)), dma((n_sec - 1,)),
             dma((n_sec - 1,)), dma((n_sec - 1,)),
-            dma((n_chip, n_sec)), dma((n_ctx, n_sec)),
-            dma((n_ctx + 1, n_sec)), dma((n_ctx + 1, n_sec)),
         ],
         compiler_params=pltpu.CompilerParams(
             collective_id=0, has_side_effects=True, vmem_limit_bytes=LIMIT
@@ -366,8 +287,7 @@
     n_ctx,
     q_ref,
     g_ref,
-    k_ref,
-    v_ref,
+    block_ref,
     att_ref,
     qg_ref,
     out_ref,
@@ -380,6 +300,7 @@
     got_part,
     final,
     gathered,
+    cache,
     sib_send,
     sib_recv,
     chip_send,
@@ -388,6 +309,10 @@
     part_recv,
     all_send,
     all_recv,
+    x_send,
+    x_recv,
+    y_send,
+    y_recv,
 ):
     sec, ctx = lax.axis_index("section"), lax.axis_index("ctx")
     chip, core = lax.div(ctx, 2), lax.rem(ctx, 2)
@@ -398,7 +323,7 @@
     part_heads = kv_heads // n_sec
     layer_count, row_count, width = q_ref.shape
     group = width // DH
-    total = k_ref.shape[0]
+    total = n_ctx * row_count
     pair = 2 * row_count
     scale = 1.0 / math.sqrt(DH)
 
@@ -409,12 +334,89 @@
         if j or c
     ]
 
+    my_rows = pl.ds(pl.multiple_of(ctx * row_count, row_count), row_count)
+
+    def rows_of(d):
+        return pl.ds(d * row_count, row_count)
+
+    def x_copy(r, h, c):
+        spot = cache.at[c, h, my_rows, :]
+        return remote(spot, spot, x_send.at[r, h, c], x_recv.at[ctx, h], (sec, 2 * r + c))
+
+    def y_copy(d, h):
+        spot = cache.at[core, h, rows_of(d), :]
+        return remote(spot, spot, y_send.at[d, h], y_recv.at[d, h], sibling)
+
+    def own_copy(h, c):
+        spot = cache.at[c, h, my_rows, :]
+        return remote(spot, spot, y_send.at[n_ctx + c, h], y_recv.at[n_ctx + c, h], sibling)
+
+    def forward(h):
+        for d in range(n_ctx - 2):
+
+            @pl.when(d < chip * 2)
+            def _():
+                spot = cache.at[core, h, rows_of(d), :]
+                remote(spot, spot, x_send.at[0, h, 0], x_recv.at[d, h], sibling).wait_recv()
+                y_copy(d, h).start()
+
+    def arrive(h):
+        for d in range(n_ctx - 2):
+
+            @pl.when(d < chip * 2)
+            def _():
+                spot = cache.at[1 - core, h, rows_of(d), :]
+                remote(spot, spot, y_send.at[d, h], y_recv.at[d, h], sibling).wait_recv()
+
+        @pl.when(core == 1)
+        def _():
+            before = pl.ds(pl.multiple_of(chip * 2 * row_count, row_count), row_count)
+            for c in range(2):
+                spot = cache.at[c, h, before, :]
+                remote(
+                    spot, spot, y_send.at[n_ctx + c, h], y_recv.at[n_ctx + c, h], sibling
+                ).wait_recv()
+
     @pl.when(step == 0)
     def _():
+        for h in range(kv_heads):
+            for c in range(2):
+                at = (c * kv_heads + h) * DH
+                cache[c, h, my_rows, :] = block_ref[:, at : at + DH]
         greet(
             [(s, d) for s, d, _, _ in others]
-            + [(sec, lax.rem(ctx + 2 * i, n_ctx)) for i in range(1, n_chip)]
-        )
+            + [
+                (sec, lax.rem(chip + i, n_chip) * 2 + c)
+                for i in range(1, n_chip)
+                for c in range(2)
+            ]
+        )
+        for h in range(kv_heads):
+            for r in range(n_chip - 1, 0, -1):
+
+                @pl.when(r > chip)
+                def _():
+                    for c in range(2):
+                        x_copy(r, h, c).start()
+
+            @pl.when(core == 0)
+            def _():
+                for c in range(2):
+                    own_copy(h, c).start()
+
+        for d in range(1, n_ctx):
+
+            @pl.when(d > ctx)
+            def _():
+                for c in range(2):
+                    for h in range(kv_heads):
+                        cache[c, h, d * row_count : (d + 1) * row_count, :] = jnp.zeros(
+                            (row_count, DH), jnp.bfloat16
+                        )
+
+        forward(0)
+
+    arrive(step)
 
     def sib_copy(h):
         return remote(send_sib.at[h], from_sib.at[h], sib_send.at[h], sib_recv.at[h], sibling)
@@ -506,8 +508,8 @@
             own = pl.ds(pl.multiple_of(core * row_count, row_count), row_count)
             gathered[:, place_of(h, core)] = final[index, own, :]
 
-    keys = k_ref[...]
-    values = v_ref[...]
+    keys = cache[0, step]
+    values = cache[1, step]
     keys_turned = keys.T
     values_turned = values.T
     key_place = lax.broadcasted_iota(jnp.int32, (total, row_count), 0)
@@ -551,6 +553,10 @@
         value_grad += jnp.dot(low, grads, preferred_element_type=jnp.float32)
         if layer == 0:
 
+            @pl.when(step < kv_heads - 1)
+            def _():
+                forward(step + 1)
+
             @pl.when(step > 0)
             def _():
                 pass_on(step - 1)
@@ -601,6 +607,24 @@
         out_ref[...] = gathered[...]
         for h in range(kv_heads):
             sib_copy(h).wait_send()
+            for r in range(1, n_chip):
+
+                @pl.when(r > chip)
+                def _():
+                    for c in range(2):
+                        x_copy(r, h, c).wait_send()
+
+            for d in range(n_ctx - 2):
+
+                @pl.when(d < chip * 2)
+                def _():
+                    y_copy(d, h).wait_send()
+
+            @pl.when(core == 0)
+            def _():
+                for c in range(2):
+                    own_copy(h, c).wait_send()
+
             for r in range(n_chip - 1):
 
                 @pl.when(r < chip)
@@ -617,25 +641,25 @@
                     all_copy(h, s, d, j, c).wait_send()
 
 
-def cross_attention(queries, cotangent, full_cache):
+def cross_attention(queries, cotangent, block):
     n_sec, n_ctx = lax.axis_size("section"), lax.axis_size("ctx")
     n_chip = n_ctx // 2
     layer_count, row_count, model_width = queries.shape
-    total, cache_width = full_cache.shape
+    cache_width = block.shape[1]
+    total = n_ctx * row_count
     kv_heads = cache_width // 2 // DH
     width = model_width // kv_heads
     pair = 2 * row_count
     part_heads = kv_heads // n_sec
     rows = pl.BlockSpec((layer_count, row_count, width), lambda h: (0, 0, h))
-    cut = pl.BlockSpec((total, DH), lambda h: (0, h))
-    cut_values = pl.BlockSpec((total, DH), lambda h: (0, kv_heads + h))
+    whole = pl.BlockSpec((row_count, cache_width), lambda h: (0, 0))
     dma = pltpu.SemaphoreType.DMA
     per_head = pltpu.VMEM((kv_heads, total, DH), jnp.bfloat16)
     return pl.pallas_call(
         functools.partial(attention_kernel, n_sec, n_ctx),
         grid=(kv_heads,),
-        in_specs=[rows, rows, cut, cut_values],
-        out_specs=[rows, rows, pl.BlockSpec((row_count, cache_width), lambda h: (0, 0))],
+        in_specs=[rows, rows, whole],
+        out_specs=[rows, rows, whole],
         out_shape=[
             jax.ShapeDtypeStruct(queries.shape, jnp.bfloat16),
             jax.ShapeDtypeStruct(queries.shape, jnp.bfloat16),
@@ -649,20 +673,23 @@
             pltpu.VMEM((n_sec, part_heads, pair, DH), jnp.bfloat16),
             pltpu.VMEM((part_heads, pair, DH), jnp.bfloat16),
             pltpu.VMEM((row_count, cache_width), jnp.bfloat16),
+            pltpu.VMEM((2, kv_heads, total, DH), jnp.bfloat16),
             dma((kv_heads,)), dma((kv_heads,)),
             dma((n_chip, kv_heads)), dma((n_chip, kv_heads)),
             dma((kv_heads,)), dma((n_sec, part_heads)),
             dma((part_heads, n_sec, 2)), dma((kv_heads, 2)),
+            dma((n_chip, kv_heads, 2)), dma((n_ctx, kv_heads)),
+            dma((n_ctx + 2, kv_heads)), dma((n_ctx + 2, kv_heads)),
         ],
         compiler_params=pltpu.CompilerParams(
             collective_id=1, has_side_effects=True, vmem_limit_bytes=LIMIT
         ),
-    )(queries, cotangent, full_cache, full_cache)
+    )(queries, cotangent, block)
 
 
 def body(queries, cotangent, ret_query, ret_key, ret_value, gate_log, kv_weight):
-    full_cache = shared_cache(ret_query, ret_key, ret_value, gate_log, kv_weight)
-    attended_all, grad_rows_all, cache_grad = cross_attention(queries, cotangent, full_cache)
+    block = shared_cache(ret_query, ret_key, ret_value, gate_log, kv_weight)
+    attended_all, grad_rows_all, cache_grad = cross_attention(queries, cotangent, block)
     retention_grad = jnp.einsum(
         "rw,cw->rc", cache_grad, kv_weight, preferred_element_type=jnp.float32
     ).astype(jnp.bfloat16)

time: 159 us -> 158 us (level)
    pallas_call x1, Pallas kernels: 83.7 us -> 107 us  [cross_attention(): pl.pallas_call(functools.partial(attention_kernel, n_sec, n_ctx), grid=(k...]
    pallas_call x1, Pallas kernels: 62.1 us -> 38.9 us  [shared_cache(): pl.pallas_call(functools.partial(cache_kernel, n_sec, n_ctx), out_shape=j...]
where the time goes in v5:
time: 158 us; the launch traced here: 156 us
  Pallas kernels  146 us (92%)
  local copies, waits for them, and re-layouts  6.28 us (4%)
  matrix products  3.11 us (2%)
    pallas_call x1, Pallas kernels, cross_attention(): pl.pallas_call(functools.partial(attention_kernel, n_sec, n_ctx), grid=(k...  107 us
    pallas_call x1, Pallas kernels, shared_cache(): pl.pallas_call(functools.partial(cache_kernel, n_sec, n_ctx), out_shape=j...  38.9 us
    unnamed x9, local copies, waits for them, and re-layouts  4.33 us

profile of v5, /device:TPU:0, one launch (start us, length us, event | category | flops | bytes accessed | tf_op | source)
XLA Modules:
  0.0 156.2 jit_solution(672589943078141859)
XLA Ops:
  0.6 1.3 pad.9.turned_ref
  1.9 0.8 copy.10
  2.7 0.6 pad.8.gate_ref
  3.4 38.9 %shard_map.94.block_ref = bf16[160,2048]{1,0:T(8,128)(2,1)} custom-call(bf16[160,768]{1,0:T(8,128)(2,1)} %q_ref.2, bf16[160,768]{1,0:T(8,128)(2,1)} %k_ref.1, bf16[160,768]{1,0:T(8,128)(2,1)} %v_ref.1, f32[160,128]{1,0:T(8,128)} %pad.8.gate_ref, f32[8,160]{1,0:T(8,128)} %pad.9.turned_ref, bf16[768,2048]{1,0:T(8,128)(2,1)} %w_ref.1), custom_call_target="tpu_custom_call" | custom-call | tf_op jit(solution)/shard_map/pallas_call | solution.py:259
  42.3 0.0 copy-start
  42.3 107.2 %shard_map.95 = (bf16[2,160,3072]{2,1,0:T(8,128)(2,1)}, bf16[2,160,3072]{2,1,0:T(8,128)(2,1)}, bf16[160,2048]{1,0:T(8,128)(2,1)}) custom-call(bf16[2,160,3072]{2,1,0:T(8,128)(2,1)} %q_ref.3, bf16[2,160,3072]{2,1,0:T(8,128)(2,1)} %g_ref.1, bf16[160,2048]{1,0:T(8,128)(2,1)} %shard_map.94.block_ref), custom_call_target="tpu_custom_call" | custom-call | tf_op jit(solution)/shard_map/pallas_call | solution.py:658
  149.5 0.0 copy-done
  149.5 0.0 copy-start.2
  149.5 3.1 %convolution_convert_fusion = bf16[160,768]{1,0:T(8,128)(2,1)} fusion(bf16[160,2048]{1,0:T(8,128)(2,1)} %get-tuple-element.8, bf16[768,2048]{1,0:T(8,128)(2,1)S(1)} %copy-done), kind=kOutput, calls=%fused_computation | convolution fusion | flops 503439360 | bytes 4046848 | tf_op jit(solution)/shard_map/rw,cw->rc/dot_general | solution.py:693
  152.6 0.0 copy-done.2
  152.6 0.0 copy-start.1
  152.6 1.3 copy.13
  153.9 1.0 copy-done.1
  154.9 1.3 copy.14
Async XLA Ops:
  42.3 107.2 %copy-start = (bf16[768,2048]{1,0:T(8,128)(2,1)S(1)}, bf16[768,2048]{1,0:T(8,128)(2,1)}, u32[]{:S(2)}) copy-start(bf16[768,2048]{1,0:T(8,128)(2,1)} %w_ref.1) | copy-start | bytes 9437188
  149.5 3.1 %copy-start.2 = (bf16[2,160,3072]{2,1,0:T(8,128)(2,1)S(1)}, bf16[2,160,3072]{2,1,0:T(8,128)(2,1)}, u32[]{:S(2)}) copy-start(bf16[2,160,3072]{2,1,0:T(8,128)(2,1)} %get-tuple-element.12) | copy-start | bytes 5898244
  152.6 2.3 %copy-start.1 = (bf16[2,160,3072]{2,1,0:T(8,128)(2,1)S(1)}, bf16[2,160,3072]{2,1,0:T(8,128)(2,1)}, u32[]{:S(2)}) copy-start(bf16[2,160,3072]{2,1,0:T(8,128)(2,1)} %get-tuple-element.13) | copy-start | bytes 5898244

commit v6 on v5

--- a/solution.py
+++ b/solution.py
@@ -351,6 +351,19 @@
         spot = cache.at[c, h, my_rows, :]
         return remote(spot, spot, y_send.at[n_ctx + c, h], y_recv.at[n_ctx + c, h], sibling)
 
+    def hand_out(h):
+        for r in range(n_chip - 1, 0, -1):
+
+            @pl.when(r > chip)
+            def _():
+                for c in range(2):
+                    x_copy(r, h, c).start()
+
+        @pl.when(core == 0)
+        def _():
+            for c in range(2):
+                own_copy(h, c).start()
+
     def forward(h):
         for d in range(n_ctx - 2):
 
@@ -391,19 +404,8 @@
                 for c in range(2)
             ]
         )
-        for h in range(kv_heads):
-            for r in range(n_chip - 1, 0, -1):
-
-                @pl.when(r > chip)
-                def _():
-                    for c in range(2):
-                        x_copy(r, h, c).start()
-
-            @pl.when(core == 0)
-            def _():
-                for c in range(2):
-                    own_copy(h, c).start()
-
+        for h in range(min(2, kv_heads)):
+            hand_out(h)
         for d in range(1, n_ctx):
 
             @pl.when(d > ctx)
@@ -552,6 +554,10 @@
         key_grad += jnp.dot(score_grad, queries, preferred_element_type=jnp.float32)
         value_grad += jnp.dot(low, grads, preferred_element_type=jnp.float32)
         if layer == 0:
+
+            @pl.when(step < kv_heads - 2)
+            def _():
+                hand_out(step + 2)
 
             @pl.when(step < kv_heads - 1)
             def _():

time: 158 us -> 151 us (0.956)
  the two profiles are of different devices: /device:TPU:0 before, /device:TPU:23 now
where the time goes in v6:
time: 151 us
  Pallas kernels  141 us (93%)
  local copies, waits for them, and re-layouts  6.28 us (4%)
  matrix products  3.11 us (2%)
    pallas_call x1, Pallas kernels, cross_attention(): pl.pallas_call(functools.partial(attention_kernel, n_sec, n_ctx), grid=(k...  94.2 us
    pallas_call x1, Pallas kernels, shared_cache(): pl.pallas_call(functools.partial(cache_kernel, n_sec, n_ctx), out_shape=j...  46.6 us
    unnamed x9, local copies, waits for them, and re-layouts  4.33 us
    dot_general x1, matrix products, body(): jnp.einsum('rw,cw->rc', cache_grad, kv_weight, preferred_element_type=jnp...  3.11 us

profile of v6, /device:TPU:23, one launch (start us, length us, event | category | flops | bytes accessed | tf_op | source)
XLA Modules:
  0.0 150.9 jit_solution(3471273018616568217)
XLA Ops:
  0.6 1.3 pad.9.turned_ref
  1.9 0.8 copy.10
  2.7 0.6 pad.8.gate_ref
  3.4 46.6 %shard_map.94.block_ref = bf16[160,2048]{1,0:T(8,128)(2,1)} custom-call(bf16[160,768]{1,0:T(8,128)(2,1)} %q_ref.2, bf16[160,768]{1,0:T(8,128)(2,1)} %k_ref.1, bf16[160,768]{1,0:T(8,128)(2,1)} %v_ref.1, f32[160,128]{1,0:T(8,128)} %pad.8.gate_ref, f32[8,160]{1,0:T(8,128)} %pad.9.turned_ref, bf16[768,2048]{1,0:T(8,128)(2,1)} %w_ref.1), custom_call_target="tpu_custom_call" | custom-call | tf_op jit(solution)/shard_map/pallas_call | solution.py:259
  50.0 0.0 copy-start
  50.0 94.2 %shard_map.95 = (bf16[2,160,3072]{2,1,0:T(8,128)(2,1)}, bf16[2,160,3072]{2,1,0:T(8,128)(2,1)}, bf16[160,2048]{1,0:T(8,128)(2,1)}) custom-call(bf16[2,160,3072]{2,1,0:T(8,128)(2,1)} %q_ref.3, bf16[2,160,3072]{2,1,0:T(8,128)(2,1)} %g_ref.1, bf16[160,2048]{1,0:T(8,128)(2,1)} %shard_map.94.block_ref), custom_call_target="tpu_custom_call" | custom-call | tf_op jit(solution)/shard_map/pallas_call | solution.py:664
  144.2 0.0 copy-done
  144.3 0.0 copy-start.2
  144.3 3.1 %convolution_convert_fusion = bf16[160,768]{1,0:T(8,128)(2,1)} fusion(bf16[160,2048]{1,0:T(8,128)(2,1)} %get-tuple-element.8, bf16[768,2048]{1,0:T(8,128)(2,1)S(1)} %copy-done), kind=kOutput, calls=%fused_computation | convolution fusion | flops 503439360 | bytes 4046848 | tf_op jit(solution)/shard_map/rw,cw->rc/dot_general | solution.py:699
  147.4 0.0 copy-done.2
  147.4 0.0 copy-start.1
  147.4 1.3 copy.13
  148.7 1.0 copy-done.1
  149.6 1.3 copy.14
Async XLA Ops:
  50.0 94.3 %copy-start = (bf16[768,2048]{1,0:T(8,128)(2,1)S(1)}, bf16[768,2048]{1,0:T(8,128)(2,1)}, u32[]{:S(2)}) copy-start(bf16[768,2048]{1,0:T(8,128)(2,1)} %w_ref.1) | copy-start | bytes 9437188
  144.3 3.1 %copy-start.2 = (bf16[2,160,3072]{2,1,0:T(8,128)(2,1)S(1)}, bf16[2,160,3072]{2,1,0:T(8,128)(2,1)}, u32[]{:S(2)}) copy-start(bf16[2,160,3072]{2,1,0:T(8,128)(2,1)} %get-tuple-element.12) | copy-start | bytes 5898244
  147.4 2.3 %copy-start.1 = (bf16[2,160,3072]{2,1,0:T(8,128)(2,1)S(1)}, bf16[2,160,3072]{2,1,0:T(8,128)(2,1)}, u32[]{:S(2)}) copy-start(bf16[2,160,3072]{2,1,0:T(8,128)(2,1)} %get-tuple-element.13) | copy-start | bytes 5898244
